TPU v7x, 256 devices: a whole 4x4x8 slice. The times are simulated.
256 devices in a mesh: ctx: 32 (over z, x), kvh: 8 (over y, core).
Axes of the slice: x: 4, y: 4, z: 8, core: 2. Of those that a mesh axis runs over, the one named last changes fastest.
Arguments:
- queries: bfloat16 [8192, 8192], P('ctx', 'kvh'), may hold values from -90 to 90
- keys: bfloat16 [8192, 1024], P('ctx', 'kvh'), may hold values from -4 to 4
- values: bfloat16 [8192, 1024], P('ctx', 'kvh'), may hold values from -6 to 6
- doc_lengths: int32 [16], replicated, may hold values from 1 to 2048, 8192 in all
Outputs:
- attended: bfloat16 [8192, 8192], P(('ctx', 'kvh'))
Inputs may be any that keep to these rules, and one draw needn't show every extreme that they name: `doc_lengths`: the lengths sum to 8192; exactly one document, or more, has length 2048.
All inputs are finite; a program needn't handle non-finite values.
Results may differ from a plain program's by a relative error of at most 0.0036.
Values may be sent and summed in bfloat16 or wider, within the bound.
No kernel may reach another device: no remote copies, remote signals or barrier semaphores. Data moves between devices by JAX's collectives and lax.ppermute only.
A program may use at most 64 MiB of HBM per device.

v0:
```python
import jax
import jax.numpy as jnp
from jax import lax
from jax.sharding import PartitionSpec as P

QUERY_PER_KEY = 8
HEAD_SIZE = 128


def passed_along(block, axis, distance):
    devices = range(lax.axis_size(axis))
    route = [(i - distance, i) for i in devices if i - distance in devices]
    return lax.ppermute(block, axis, route)


def doc_of(positions, starts):
    return jnp.sum((starts[None, :] <= positions[:, None]).astype(jnp.int32), axis=1) - 1


def per_device(queries, keys, values, doc_lengths):
    rows = keys.shape[0]
    scale = 1.0 / HEAD_SIZE**0.5
    span = min(8, lax.axis_size("ctx") // 2)
    place = lax.axis_index("ctx")
    paired = jnp.stack([keys, values])
    pieces = []
    for step in range(span, 0, -1):
        pieces.append(passed_along(paired, "ctx", step))
    window = jnp.concatenate(pieces + [paired], axis=1)
    width = window.shape[1]
    starts = jnp.cumsum(doc_lengths) - doc_lengths
    query_pos = place * rows + jnp.arange(rows, dtype=jnp.int32)
    key_pos = (place - span) * rows + jnp.arange(width, dtype=jnp.int32)
    allowed = (doc_of(key_pos, starts)[None, :] == doc_of(query_pos, starts)[:, None]) & (
        key_pos[None, :] <= query_pos[:, None]
    )
    outputs = []
    key_head = window[0, :, 0:HEAD_SIZE]
    value_head = window[1, :, 0:HEAD_SIZE]
    for inner_loop in range(QUERY_PER_KEY):
        query_head = queries[:, inner_loop * HEAD_SIZE : (inner_loop + 1) * HEAD_SIZE]
        score = (
            jnp.einsum("qd,kd->qk", query_head, key_head, preferred_element_type=jnp.float32)
            * scale
        )
        score = jnp.where(allowed, score, jnp.float32(-1e30))
        top = jnp.max(score, axis=1, keepdims=True)
        weight = jnp.where(allowed, jnp.exp(score - top), jnp.float32(0.0))
        total = jnp.sum(weight, axis=1, keepdims=True)
        prob = weight.astype(jnp.bfloat16)
        mixed = jnp.dot(prob, value_head, preferred_element_type=jnp.float32) / total
        outputs.append(mixed.astype(jnp.bfloat16))
    attended = jnp.concatenate(outputs, axis=1)
    return lax.all_to_all(attended, "kvh", split_axis=0, concat_axis=1, tiled=True)


def solution(mesh):
    in_specs = (P("ctx", "kvh"), P("ctx", "kvh"), P("ctx", "kvh"), P())
    out_specs = P(("ctx", "kvh"), None)
    return jax.shard_map(
        per_device, mesh=mesh, in_specs=in_specs, out_specs=out_specs, check_vma=False
    )
```

profile of v0, /device:TPU:96, one launch (start us, length us, event | category | flops | bytes accessed | tf_op | source)
XLA Modules:
  0.0 79.3 jit_solution(15171735292873014370)
XLA Ops:
  0.0 1.0 %pad_maximum_fusion = bf16[2,256,128]{2,1,0:T(8,128)(2,1)S(1)} fusion(bf16[1,256,128]{2,1,0:T(8,128)(2,1)} %bitcast.77, bf16[1,256,128]{2,1,0:T(8,128)(2,1)} %bitcast.79), kind=kLoop, calls=%fused_computation.100 | loop fusion | flops 65536 | bytes 262144 | tf_op jit(solution)/shard_map/stack | solution.py:25
  1.0 5.5 %collective-permute-start = (bf16[2,256,128]{2,1,0:T(8,128)(2,1)S(1)}, bf16[2,256,128]{2,1,0:T(8,128)(2,1)S(1)}, u32[]{:S(2)}, u32[]{:S(2)}) collective-permute-start(bf16[2,256,128]{2,1,0:T(8,128)(2,1)S(1)} %pad_maximum_fusion), channel_id=1, source_target_pairs={{0,64},{8,72},{16,80},{24,88},{32,96},{40,104},{48,112},{56,120},{... | collective-permute-start | bytes 393224 | tf_op jit(solution)/shard_map/ppermute | solution.py:13
  6.5 5.1 %collective-permute-start.1 = (bf16[2,256,128]{2,1,0:T(8,128)(2,1)S(1)}, bf16[2,256,128]{2,1,0:T(8,128)(2,1)S(1)}, u32[]{:S(2)}, u32[]{:S(2)}) collective-permute-start(bf16[2,256,128]{2,1,0:T(8,128)(2,1)S(1)} %pad_maximum_fusion), channel_id=1, source_target_pairs={{0,56},{8,64},{16,72},{24,80},{32,88},{40,96},{48,104},{56,112},{6... | collective-permute-start | bytes 393224 | tf_op jit(solution)/shard_map/ppermute | solution.py:13
  11.6 2.2 %collective-permute-start.2 = (bf16[2,256,128]{2,1,0:T(8,128)(2,1)S(1)}, bf16[2,256,128]{2,1,0:T(8,128)(2,1)S(1)}, u32[]{:S(2)}, u32[]{:S(2)}) collective-permute-start(bf16[2,256,128]{2,1,0:T(8,128)(2,1)S(1)} %pad_maximum_fusion), channel_id=1, source_target_pairs={{0,48},{8,56},{16,64},{24,72},{32,80},{40,88},{48,96},{56,104},{64... | collective-permute-start | bytes 393224 | tf_op jit(solution)/shard_map/ppermute | solution.py:13
  13.8 3.0 %collective-permute-start.3 = (bf16[2,256,128]{2,1,0:T(8,128)(2,1)S(1)}, bf16[2,256,128]{2,1,0:T(8,128)(2,1)S(1)}, u32[]{:S(2)}, u32[]{:S(2)}) collective-permute-start(bf16[2,256,128]{2,1,0:T(8,128)(2,1)S(1)} %pad_maximum_fusion), channel_id=1, source_target_pairs={{0,40},{8,48},{16,56},{24,64},{32,72},{40,80},{48,88},{56,96},{64,... | collective-permute-start | bytes 393224 | tf_op jit(solution)/shard_map/ppermute | solution.py:13
  16.7 1.9 %collective-permute-start.4 = (bf16[2,256,128]{2,1,0:T(8,128)(2,1)S(1)}, bf16[2,256,128]{2,1,0:T(8,128)(2,1)S(1)}, u32[]{:S(2)}, u32[]{:S(2)}) collective-permute-start(bf16[2,256,128]{2,1,0:T(8,128)(2,1)S(1)} %pad_maximum_fusion), channel_id=1, source_target_pairs={{0,32},{8,40},{16,48},{24,56},{32,64},{40,72},{48,80},{56,88},{64,... | collective-permute-start | bytes 393224 | tf_op jit(solution)/shard_map/ppermute | solution.py:13
  20.5 3.7 %collective-permute-start.5 = (bf16[2,256,128]{2,1,0:T(8,128)(2,1)S(1)}, bf16[2,256,128]{2,1,0:T(8,128)(2,1)S(1)}, u32[]{:S(2)}, u32[]{:S(2)}) collective-permute-start(bf16[2,256,128]{2,1,0:T(8,128)(2,1)S(1)} %pad_maximum_fusion), channel_id=1, source_target_pairs={{0,24},{8,32},{16,40},{24,48},{32,56},{40,64},{48,72},{56,80},{64,... | collective-permute-start | bytes 393224 | tf_op jit(solution)/shard_map/ppermute | solution.py:13
  24.2 3.8 %collective-permute-start.6 = (bf16[2,256,128]{2,1,0:T(8,128)(2,1)S(1)}, bf16[2,256,128]{2,1,0:T(8,128)(2,1)S(1)}, u32[]{:S(2)}, u32[]{:S(2)}) collective-permute-start(bf16[2,256,128]{2,1,0:T(8,128)(2,1)S(1)} %pad_maximum_fusion), channel_id=1, source_target_pairs={{0,16},{8,24},{16,32},{24,40},{32,48},{40,56},{48,64},{56,72},{64,... | collective-permute-start | bytes 393224 | tf_op jit(solution)/shard_map/ppermute | solution.py:13
  28.0 3.3 %collective-permute-start.7 = (bf16[2,256,128]{2,1,0:T(8,128)(2,1)S(1)}, bf16[2,256,128]{2,1,0:T(8,128)(2,1)S(1)}, u32[]{:S(2)}, u32[]{:S(2)}) collective-permute-start(bf16[2,256,128]{2,1,0:T(8,128)(2,1)S(1)} %pad_maximum_fusion), channel_id=1, source_target_pairs={{0,8},{8,16},{16,24},{24,32},{32,40},{40,48},{48,56},{56,64},{64,7... | collective-permute-start | bytes 393224 | tf_op jit(solution)/shard_map/ppermute | solution.py:13
  31.5 7.0 %collective-permute-done.6 = bf16[2,256,128]{2,1,0:T(8,128)(2,1)S(1)} collective-permute-done((bf16[2,256,128]{2,1,0:T(8,128)(2,1)S(1)}, bf16[2,256,128]{2,1,0:T(8,128)(2,1)S(1)}, u32[]{:S(2)}, u32[]{:S(2)}) %collective-permute-start.6) | collective-permute-done | bytes 131104 | tf_op jit(solution)/shard_map/ppermute | solution.py:13
  38.5 5.2 %collective-permute-done.7 = bf16[2,256,128]{2,1,0:T(8,128)(2,1)S(1)} collective-permute-done((bf16[2,256,128]{2,1,0:T(8,128)(2,1)S(1)}, bf16[2,256,128]{2,1,0:T(8,128)(2,1)S(1)}, u32[]{:S(2)}, u32[]{:S(2)}) %collective-permute-start.7) | collective-permute-done | bytes 131104 | tf_op jit(solution)/shard_map/ppermute | solution.py:13
  45.3 0.8 fusion.155
  49.8 3.9 %fusion.30 = (f32[256]{0:T(256)S(1)}, f32[256]{0:T(256)S(1)}, f32[256]{0:T(256)S(1)}, f32[256]{0:T(256)S(1)}, f32[256]{0:T(256)S(1)}, /*index=5*/f32[256]{0:T(256)S(1)}, f32[256]{0:T(256)S(1)}) fusion(f32[256,2304]{0,1:T(8,128)S(1)} %get-tuple-element.15, f32[256]{0:T(256)S(1)} %get-tuple-element.14, s32[256]{0:T(256)S(1)} %iota_add_fusion.1, ...), kind=kLoop, calls=%fused_computation.47 | loop fusion | flops 14153984 | bytes 16549888 | tf_op jit(solution)/shard_map/reduce_sum | solution.py:49
  53.7 1.0 %fusion.112 = bf16[256,1024]{0,1:T(8,128)(2,1)S(1)} fusion(f32[256,2304]{0,1:T(8,128)S(1)} %get-tuple-element.13, f32[256]{0:T(256)S(1)} %get-tuple-element.12, bf16[2,2304,128]{2,1,0:T(8,128)(2,1)S(1)} %constant_dynamic-update-slice_fusion, f32[256]{0:T(256)S(1)} %get-tuple-element.6, s32[256]{0:T(256)S(1)} %iota_add_fusion.1, ...), kind=kOutput, calls=%fused_computation.89 | convolution fusion | flops 154599424 | bytes 3043328 | tf_op jit(solution)/shard_map/dot_general | solution.py:51
  54.7 1.0 %fusion.115 = bf16[256,1024]{0,1:T(8,128)(2,1)S(1)} fusion(bf16[256,1024]{0,1:T(8,128)(2,1)S(1)} %fusion.112, f32[256,2304]{0,1:T(8,128)S(1)} %get-tuple-element.17, f32[256]{0:T(256)S(1)} %get-tuple-element.16, bf16[2,2304,128]{2,1,0:T(8,128)(2,1)S(1)} %constant_dynamic-update-slice_fusion, f32[256]{0:T(256)S(1)} %get-tuple-element.7, ...), kind=kOutput, calls=%fused_computation.90 | convolution fusion | flops 154599424 | bytes 3043328 | tf_op jit(solution)/shard_map/dot_general | solution.py:51
  55.8 1.0 %fusion.118 = bf16[256,1024]{0,1:T(8,128)(2,1)S(1)} fusion(bf16[256,1024]{0,1:T(8,128)(2,1)S(1)} %fusion.115, f32[256,2304]{0,1:T(8,128)S(1)} %get-tuple-element.19, f32[256]{0:T(256)S(1)} %get-tuple-element.18, bf16[2,2304,128]{2,1,0:T(8,128)(2,1)S(1)} %constant_dynamic-update-slice_fusion, f32[256]{0:T(256)S(1)} %get-tuple-element.8, ...), kind=kOutput, calls=%fused_computation.91 | convolution fusion | flops 154599424 | bytes 3043328 | tf_op jit(solution)/shard_map/dot_general | solution.py:51
  56.9 1.0 %fusion.121 = bf16[256,1024]{0,1:T(8,128)(2,1)S(1)} fusion(bf16[256,1024]{0,1:T(8,128)(2,1)S(1)} %fusion.118, f32[256,2304]{0,1:T(8,128)S(1)} %get-tuple-element.21, f32[256]{0:T(256)S(1)} %get-tuple-element.20, bf16[2,2304,128]{2,1,0:T(8,128)(2,1)S(1)} %constant_dynamic-update-slice_fusion, f32[256]{0:T(256)S(1)} %get-tuple-element.9, ...), kind=kOutput, calls=%fused_computation.92 | convolution fusion | flops 154599424 | bytes 3043328 | tf_op jit(solution)/shard_map/dot_general | solution.py:51
  57.9 1.0 %fusion.124 = bf16[256,1024]{0,1:T(8,128)(2,1)S(1)} fusion(bf16[256,1024]{0,1:T(8,128)(2,1)S(1)} %fusion.121, f32[256,2304]{0,1:T(8,128)S(1)} %get-tuple-element.23, f32[256]{0:T(256)S(1)} %get-tuple-element.22, bf16[2,2304,128]{2,1,0:T(8,128)(2,1)S(1)} %constant_dynamic-update-slice_fusion, f32[256]{0:T(256)S(1)} %get-tuple-element.10, ...), kind=kOutput, calls=%fused_computation.93 | convolution fusion | flops 154599424 | bytes 3043328 | tf_op jit(solution)/shard_map/dot_general | solution.py:51
  59.0 1.0 %fusion.127 = bf16[256,1024]{0,1:T(8,128)(2,1)S(1)} fusion(bf16[256,1024]{0,1:T(8,128)(2,1)S(1)} %fusion.124, f32[256,2304]{0,1:T(8,128)S(1)} %get-tuple-element.25, f32[256]{0:T(256)S(1)} %get-tuple-element.24, bf16[2,2304,128]{2,1,0:T(8,128)(2,1)S(1)} %constant_dynamic-update-slice_fusion, f32[256]{0:T(256)S(1)} %get-tuple-element.11, ...), kind=kOutput, calls=%fused_computation.94 | convolution fusion | flops 154599424 | bytes 3043328 | tf_op jit(solution)/shard_map/dot_general | solution.py:51
  60.0 1.4 %fusion.28 = f32[256]{0:T(256)S(1)} fusion(f32[256,2304]{0,1:T(8,128)S(1)} %get-tuple-element.27, f32[256]{0:T(256)S(1)} %get-tuple-element.26, s32[256]{0:T(256)S(1)} %iota_add_fusion.1, s32[2304]{0:T(1024)S(1)} %iota_add_fusion, s32[256]{0:T(256)S(1)} %broadcast_add_fusion.1, s32[2304]{0:T(1024)S(1)} %broadcast_add_fusion), kind=kLoop, calls=%fused_computation.45 | loop fusion | flops 3538688 | bytes 2381824 | tf_op jit(solution)/shard_map/reduce_sum | solution.py:49
  61.4 1.0 %fusion.130 = bf16[256,1024]{0,1:T(8,128)(2,1)S(1)} fusion(bf16[256,1024]{0,1:T(8,128)(2,1)S(1)} %fusion.127, f32[256,2304]{0,1:T(8,128)S(1)} %get-tuple-element.27, f32[256]{0:T(256)S(1)} %get-tuple-element.26, bf16[2,2304,128]{2,1,0:T(8,128)(2,1)S(1)} %constant_dynamic-update-slice_fusion, f32[256]{0:T(256)S(1)} %fusion.28, s32[256]{0:T(256)S(1)} %iota_add_fusion.1, ...), kind=kOutput, calls=%fused_computation.95 | convolution fusion | flops 154599424 | bytes 3043328 | tf_op jit(solution)/shard_map/dot_general | solution.py:51
  62.5 1.0 %fusion.133 = bf16[256,1024]{0,1:T(8,128)(2,1)S(1)} fusion(bf16[256,1024]{0,1:T(8,128)(2,1)S(1)} %fusion.130, f32[256,2304]{0,1:T(8,128)S(1)} %get-tuple-element.15, f32[256]{0:T(256)S(1)} %get-tuple-element.14, bf16[2,2304,128]{2,1,0:T(8,128)(2,1)S(1)} %constant_dynamic-update-slice_fusion, f32[256]{0:T(256)S(1)} %get-tuple-element.5, ...), kind=kOutput, calls=%fused_computation.96 | convolution fusion | flops 154599424 | bytes 3043328 | tf_op jit(solution)/shard_map/dot_general | solution.py:51
  63.8 14.7 %all_to_all.19 = bf16[8,32,1024]{2,1,0:T(8,128)(2,1)S(1)} all-to-all(bf16[8,32,1024]{2,1,0:T(8,128)(2,1)S(1)} %bitcast.75), channel_id=1, replica_groups=mesh['ctx'=32,'kvh'=8] {'kvh'}, dimensions={0} | all-to-all | bytes 1048576 | tf_op jit(solution)/shard_map/all_to_all | solution.py:54
  78.4 0.8 %copy.15 = bf16[8,4,8,1024]{3,2,0,1:T(8,128)(2,1)} copy(bf16[8,4,8,1024]{3,2,1,0:T(8,128)(2,1)S(1)} %bitcast.76) | data formatting | bytes 1048576 | tf_op jit(solution)/shard_map/all_to_all | solution.py:54
  (39 shorter events, 7.4 us)
Async XLA Ops:
  0.0 43.7 %copy-start.1 = (bf16[256,128]{1,0:T(8,128)(2,1)S(1)}, bf16[256,128]{1,0:T(8,128)(2,1)}, u32[]{:S(2)}) copy-start(bf16[256,128]{1,0:T(8,128)(2,1)} %param.5) | copy-start | bytes 196612
  0.0 43.7 %copy-start = (bf16[256,128]{1,0:T(8,128)(2,1)S(1)}, bf16[256,128]{1,0:T(8,128)(2,1)}, u32[]{:S(2)}) copy-start(bf16[256,128]{1,0:T(8,128)(2,1)} %param.6) | copy-start | bytes 196612
  0.0 43.8 %copy-start.2 = (bf16[256,1024]{1,0:T(8,128)(2,1)S(1)}, bf16[256,1024]{1,0:T(8,128)(2,1)}, u32[]{:S(2)}) copy-start(bf16[256,1024]{1,0:T(8,128)(2,1)} %param.4) | copy-start | bytes 1572868
  1.0 19.5 %collective-permute-start = (bf16[2,256,128]{2,1,0:T(8,128)(2,1)S(1)}, bf16[2,256,128]{2,1,0:T(8,128)(2,1)S(1)}, u32[]{:S(2)}, u32[]{:S(2)}) collective-permute-start(bf16[2,256,128]{2,1,0:T(8,128)(2,1)S(1)} %pad_maximum_fusion), channel_id=1, source_target_pairs={{0,64},{8,72},{16,80},{24,88},{32,96},{40,104},{48,112},{56,120},{... | collective-permute-start | bytes 393224 | tf_op jit(solution)/shard_map/ppermute | solution.py:13
  6.5 17.7 %collective-permute-start.1 = (bf16[2,256,128]{2,1,0:T(8,128)(2,1)S(1)}, bf16[2,256,128]{2,1,0:T(8,128)(2,1)S(1)}, u32[]{:S(2)}, u32[]{:S(2)}) collective-permute-start(bf16[2,256,128]{2,1,0:T(8,128)(2,1)S(1)} %pad_maximum_fusion), channel_id=1, source_target_pairs={{0,56},{8,64},{16,72},{24,80},{32,88},{40,96},{48,104},{56,112},{6... | collective-permute-start | bytes 393224 | tf_op jit(solution)/shard_map/ppermute | solution.py:13
  11.6 16.4 %collective-permute-start.2 = (bf16[2,256,128]{2,1,0:T(8,128)(2,1)S(1)}, bf16[2,256,128]{2,1,0:T(8,128)(2,1)S(1)}, u32[]{:S(2)}, u32[]{:S(2)}) collective-permute-start(bf16[2,256,128]{2,1,0:T(8,128)(2,1)S(1)} %pad_maximum_fusion), channel_id=1, source_target_pairs={{0,48},{8,56},{16,64},{24,72},{32,80},{40,88},{48,96},{56,104},{64... | collective-permute-start | bytes 393224 | tf_op jit(solution)/shard_map/ppermute | solution.py:13
  13.8 17.6 %collective-permute-start.3 = (bf16[2,256,128]{2,1,0:T(8,128)(2,1)S(1)}, bf16[2,256,128]{2,1,0:T(8,128)(2,1)S(1)}, u32[]{:S(2)}, u32[]{:S(2)}) collective-permute-start(bf16[2,256,128]{2,1,0:T(8,128)(2,1)S(1)} %pad_maximum_fusion), channel_id=1, source_target_pairs={{0,40},{8,48},{16,56},{24,64},{32,72},{40,80},{48,88},{56,96},{64,... | collective-permute-start | bytes 393224 | tf_op jit(solution)/shard_map/ppermute | solution.py:13
  16.7 14.6 %collective-permute-start.4 = (bf16[2,256,128]{2,1,0:T(8,128)(2,1)S(1)}, bf16[2,256,128]{2,1,0:T(8,128)(2,1)S(1)}, u32[]{:S(2)}, u32[]{:S(2)}) collective-permute-start(bf16[2,256,128]{2,1,0:T(8,128)(2,1)S(1)} %pad_maximum_fusion), channel_id=1, source_target_pairs={{0,32},{8,40},{16,48},{24,56},{32,64},{40,72},{48,80},{56,88},{64,... | collective-permute-start | bytes 393224 | tf_op jit(solution)/shard_map/ppermute | solution.py:13
  20.5 10.9 %collective-permute-start.5 = (bf16[2,256,128]{2,1,0:T(8,128)(2,1)S(1)}, bf16[2,256,128]{2,1,0:T(8,128)(2,1)S(1)}, u32[]{:S(2)}, u32[]{:S(2)}) collective-permute-start(bf16[2,256,128]{2,1,0:T(8,128)(2,1)S(1)} %pad_maximum_fusion), channel_id=1, source_target_pairs={{0,24},{8,32},{16,40},{24,48},{32,56},{40,64},{48,72},{56,80},{64,... | collective-permute-start | bytes 393224 | tf_op jit(solution)/shard_map/ppermute | solution.py:13
  24.2 14.3 %collective-permute-start.6 = (bf16[2,256,128]{2,1,0:T(8,128)(2,1)S(1)}, bf16[2,256,128]{2,1,0:T(8,128)(2,1)S(1)}, u32[]{:S(2)}, u32[]{:S(2)}) collective-permute-start(bf16[2,256,128]{2,1,0:T(8,128)(2,1)S(1)} %pad_maximum_fusion), channel_id=1, source_target_pairs={{0,16},{8,24},{16,32},{24,40},{32,48},{40,56},{48,64},{56,72},{64,... | collective-permute-start | bytes 393224 | tf_op jit(solution)/shard_map/ppermute | solution.py:13
  28.0 15.7 %collective-permute-start.7 = (bf16[2,256,128]{2,1,0:T(8,128)(2,1)S(1)}, bf16[2,256,128]{2,1,0:T(8,128)(2,1)S(1)}, u32[]{:S(2)}, u32[]{:S(2)}) collective-permute-start(bf16[2,256,128]{2,1,0:T(8,128)(2,1)S(1)} %pad_maximum_fusion), channel_id=1, source_target_pairs={{0,8},{8,16},{16,24},{24,32},{32,40},{40,48},{48,56},{56,64},{64,7... | collective-permute-start | bytes 393224 | tf_op jit(solution)/shard_map/ppermute | solution.py:13
where the time goes:
time: 79.6 us; the launch traced here: 79.3 us
  starting transfers between devices  28.4 us (36%)
  blocking collectives  14.7 us (18%)
  matrix products  14.4 us (18%)
  waiting for transfers between devices  12.3 us (15%)
  other arithmetic  7.35 us (9%)
  local copies, waits for them, and re-layouts  1.94 us (2%)
    ppermute x8, starting transfers between devices, passed_along(): return lax.ppermute(block, axis, route)  28.4 us
    all_to_all x1, blocking collectives, per_device(): lax.all_to_all(attended, 'kvh', split_axis=0, concat_axis=1, tiled=True)  14.7 us
    ppermute x8, waiting for transfers between devices, passed_along(): return lax.ppermute(block, axis, route)  12.3 us
    dot_general x8, matrix products, per_device(): jnp.dot(prob, value_head, preferred_element_type=jnp.float32) / total  8.36 us
    dot_general x8, matrix products, per_device(): jnp.einsum('qd,kd->qk', query_head, key_head, preferred_element_type=jnp....  5.99 us
    reduce_sum x2, other arithmetic, per_device(): total = jnp.sum(weight, axis=1, keepdims=True)  5.35 us
  transfers between devices with their start and end apart: 8, of which 2 were waited for; matrix products, arithmetic and copies ran while one was open for 2% of the time, Pallas kernels for 0%

commit v1 on v0

v1 whole, which is shorter than its diff:
```python
import functools

import jax
import jax.numpy as jnp
from jax import lax
from jax.experimental import pallas as pl
from jax.experimental.pallas import tpu as pltpu
from jax.sharding import PartitionSpec as P

HEADS = 8
DIM = 128
ROWS = 256
NDOCS = 16
NX = 4
BIG = float(2**18)
SCALE = 1.0 / DIM**0.5
F32 = jnp.float32
BF16 = jnp.bfloat16


def bounds(len_ref):
    lane = lax.broadcasted_iota(jnp.int32, (1, DIM), 1)
    first = jnp.full((1, DIM), 2**30, jnp.int32)
    last = jnp.full((1, DIM), 2**30, jnp.int32)
    first = jnp.where(lane == NDOCS, -(2**30), first)
    last = jnp.where(lane == NDOCS, 0, last)
    at = jnp.int32(0)
    for d in range(NDOCS):
        first = jnp.where(lane == d, at, first)
        at = at + len_ref[d]
        last = jnp.where(lane == d, at, last)
    return first, last


def member(first, last, start):
    pos = start + lax.broadcasted_iota(jnp.int32, (ROWS, DIM), 0)
    return (pos >= first) & (pos < last)


def attend(kinds, has_state, final, *refs):
    n = len(kinds)
    len_ref, place_ref, q_ref = refs[:3]
    kv = refs[3 : 3 + n]
    rest = refs[3 + n :]
    if has_state:
        acc_in, tot_in, top_in = rest[:3]
        rest = rest[3:]
    if final:
        out_ref, qa_ref, ka_ref, va_ref = rest
    else:
        acc_out, tot_out, top_out, qa_ref, ka_ref, va_ref = rest
    place = place_ref[0]
    x = lax.rem(place, NX)
    row = place - x
    first, last = bounds(len_ref)
    qa_ref[...] = jnp.where(member(first, last, place * ROWS), 0.0, -BIG).astype(BF16)
    for b, (kind, d) in enumerate(kinds):
        if kind == "own":
            block = place
        elif kind == "z":
            block = place - NX * d
        elif kind == "row":
            block = row - NX + (x ^ d)
        else:
            other = x ^ d
            block = jnp.where(other < x, row, row - 2 * NX) + other
        rows = slice(b * ROWS, (b + 1) * ROWS)
        ka_ref[rows, :DIM] = kv[b][0]
        ka_ref[rows, DIM:] = jnp.where(member(first, last, block * ROWS), 1.0, 0.0).astype(BF16)
        va_ref[rows, :DIM] = kv[b][1]
        va_ref[rows, DIM:] = jnp.ones((ROWS, DIM), BF16)
    for h in range(HEADS):
        qq = jnp.concatenate([q_ref[:, h * DIM : (h + 1) * DIM], qa_ref[...]], axis=1)
        s = lax.dot_general(qq, ka_ref[...], (((1,), (1,)), ((), ())), preferred_element_type=F32)
        parts = []
        for b, (kind, _) in enumerate(kinds):
            c = s[:, b * ROWS : (b + 1) * ROWS]
            if kind == "own":
                r_id = lax.broadcasted_iota(jnp.int32, (ROWS, ROWS), 0)
                c_id = lax.broadcasted_iota(jnp.int32, (ROWS, ROWS), 1)
                c = jnp.where(c_id <= r_id, c, -BIG)
            parts += [c[:, :DIM], c[:, DIM:]]
        top = parts[0]
        for c in parts[1:]:
            top = jnp.maximum(top, c)
        top = jnp.broadcast_to(jnp.max(top, axis=1, keepdims=True), (ROWS, DIM))
        if has_state:
            old = top_in[h]
            top = jnp.maximum(old, top)
            keep = jnp.exp((old - top) * SCALE)
        p = jnp.concatenate([jnp.exp((c - top) * SCALE).astype(BF16) for c in parts], axis=1)
        mixed = jnp.dot(p, va_ref[...], preferred_element_type=F32)
        acc, tot = mixed[:, :DIM], mixed[:, DIM:]
        if has_state:
            acc = acc + acc_in[h] * keep
            tot = tot + tot_in[h] * keep
        if final:
            out_ref[:, h * DIM : (h + 1) * DIM] = (acc / tot).astype(BF16)
        else:
            acc_out[h] = acc
            tot_out[h] = tot
            top_out[h] = top


def attend_part(lengths, place, queries, parts, state=None, final=False):
    kinds = tuple(k for k, _ in parts)
    n = len(kinds)
    vmem = pl.BlockSpec(memory_space=pltpu.VMEM)
    smem = pl.BlockSpec(memory_space=pltpu.SMEM)
    arrays = [queries] + [a for _, a in parts] + list(state or ())
    part = jax.ShapeDtypeStruct((HEADS, ROWS, DIM), F32)
    out = jax.ShapeDtypeStruct((ROWS, HEADS * DIM), BF16)
    return pl.pallas_call(
        functools.partial(attend, kinds, state is not None, final),
        out_shape=out if final else (part,) * 3,
        in_specs=[smem, smem] + [vmem] * len(arrays),
        out_specs=vmem if final else (vmem,) * 3,
        scratch_shapes=[
            pltpu.VMEM((ROWS, DIM), BF16),
            pltpu.VMEM((n * ROWS, 2 * DIM), BF16),
            pltpu.VMEM((n * ROWS, 2 * DIM), BF16),
        ],
        cost_estimate=pl.CostEstimate(
            flops=8 * HEADS * ROWS * ROWS * DIM * n,
            bytes_accessed=1 << 20,
            transcendentals=HEADS * ROWS * ROWS * n,
        ),
        compiler_params=pltpu.CompilerParams(vmem_limit_bytes=40 * 2**20),
        name="attend",
    )(lengths, place, *arrays)


def per_device(queries, keys, values, doc_lengths):
    size = lax.axis_size("ctx")
    down = [(i, (i + NX) % size) for i in range(size)]
    flips = {d: [(i, i ^ d) for i in range(size)] for d in (1, 2, 3)}
    place = lax.axis_index("ctx")
    x = place % NX
    where = place.astype(jnp.int32).reshape(1)
    own = jnp.stack([keys, values])
    one = lax.ppermute(own, "ctx", down)
    row = {d: lax.ppermute(one, "ctx", flips[d]) for d in (2, 1, 3)}
    two = lax.ppermute(one, "ctx", down)
    mix = {}
    for d in (2, 1, 3):
        mix[d] = lax.ppermute(jnp.where(x < (x ^ d), own, two), "ctx", flips[d])
    parts = (
        [(("own", 0), own), (("z", 1), one), (("z", 2), two)]
        + [(("row", d), row[d]) for d in (1, 3, 2)]
        + [(("mix", d), mix[d]) for d in (1, 3, 2)]
    )
    attended = attend_part(doc_lengths, where, queries, parts, None, True)
    return lax.all_to_all(attended, "kvh", split_axis=0, concat_axis=1, tiled=True)


def solution(mesh):
    in_specs = (P("ctx", "kvh"), P("ctx", "kvh"), P("ctx", "kvh"), P())
    out_specs = P(("ctx", "kvh"), None)
    return jax.shard_map(
        per_device, mesh=mesh, in_specs=in_specs, out_specs=out_specs, check_vma=False
    )
```

time: 79.6 us -> 49.4 us (0.62)
  the two profiles are of different devices: /device:TPU:96 before, /device:TPU:1 now
where the time goes in v1:
time: 49.4 us; the launch traced here: 49.3 us
  blocking collectives  16 us (32%)
  waiting for transfers between devices  14.1 us (29%)
  starting transfers between devices  9.85 us (20%)
  Pallas kernels  7.41 us (15%)
  other arithmetic  0.98 us (2%)
  local copies, waits for them, and re-layouts  0.85 us (2%)
    all_to_all x1, blocking collectives, per_device(): lax.all_to_all(attended, 'kvh', split_axis=0, concat_axis=1, tiled=True)  16 us
    pallas_call x1, Pallas kernels, attend_part(): pl.pallas_call(functools.partial(attend, kinds, state is not None, final)...  7.41 us
    ppermute x1, waiting for transfers between devices, per_device(): one = lax.ppermute(own, 'ctx', down)  7.16 us
    ppermute x3, waiting for transfers between devices, per_device(): mix[d] = lax.ppermute(jnp.where(x < x ^ d, own, two), 'ctx', flips[d])  5.37 us
    ppermute x3, starting transfers between devices, per_device(): mix[d] = lax.ppermute(jnp.where(x < x ^ d, own, two), 'ctx', flips[d])  3.69 us
    ppermute x3, starting transfers between devices, per_device(): row = {d: lax.ppermute(one, 'ctx', flips[d]) for d in (2, 1, 3)}  3.61 us
    ppermute x1, starting transfers between devices, per_device(): one = lax.ppermute(own, 'ctx', down)  2.54 us
    ppermute x1, waiting for transfers between devices, per_device(): two = lax.ppermute(one, 'ctx', down)  1.42 us
  transfers between devices with their start and end apart: 8, of which 5 were waited for; matrix products, arithmetic and copies ran while one was open for 0% of the time, Pallas kernels for 0%

profile of v1, /device:TPU:1, one launch (start us, length us, event | category | flops | bytes accessed | tf_op | source)
XLA Modules:
  0.0 49.3 jit_solution(7779717899760824916)
XLA Ops:
  0.0 1.0 %pad_maximum_fusion.refs_3_ = bf16[2,256,128]{2,1,0:T(8,128)(2,1)S(1)} fusion(bf16[1,256,128]{2,1,0:T(8,128)(2,1)} %bitcast.9, bf16[1,256,128]{2,1,0:T(8,128)(2,1)} %bitcast.11), kind=kLoop, calls=%fused_computation | loop fusion | flops 65536 | bytes 262144 | tf_op jit(solution)/shard_map/stack | solution.py:140
  1.0 2.5 %collective-permute-start = (bf16[2,256,128]{2,1,0:T(8,128)(2,1)S(1)}, bf16[2,256,128]{2,1,0:T(8,128)(2,1)S(1)}, u32[]{:S(2)}, u32[]{:S(2)}) collective-permute-start(bf16[2,256,128]{2,1,0:T(8,128)(2,1)S(1)} %pad_maximum_fusion.refs_3_), channel_id=1, source_target_pairs={{0,32},{8,40},{16,48},{24,56},{32,64},{40,72},{48,80},{56,88},{64,... | collective-permute-start | bytes 393224 | tf_op jit(solution)/shard_map/ppermute | solution.py:141
  3.5 7.2 %collective-permute-done.refs_4_ = bf16[2,256,128]{2,1,0:T(8,128)(2,1)S(1)} collective-permute-done((bf16[2,256,128]{2,1,0:T(8,128)(2,1)S(1)}, bf16[2,256,128]{2,1,0:T(8,128)(2,1)S(1)}, u32[]{:S(2)}, u32[]{:S(2)}) %collective-permute-start) | collective-permute-done | bytes 131104 | tf_op jit(solution)/shard_map/ppermute | solution.py:141
  10.7 0.0 collective-permute-start.1
  10.7 2.7 %collective-permute-start.4 = (bf16[2,256,128]{2,1,0:T(8,128)(2,1)S(1)}, bf16[2,256,128]{2,1,0:T(8,128)(2,1)S(1)}, u32[]{:S(2)}, u32[]{:S(2)}) collective-permute-start(bf16[2,256,128]{2,1,0:T(8,128)(2,1)S(1)} %collective-permute-done.refs_4_), channel_id=1, source_target_pairs={{0,16},{8,24},{16,0},{24,8},{32,48},{40,56},{48,32},{56,40},{64,80... | collective-permute-start | bytes 393224 | tf_op jit(solution)/shard_map/ppermute | solution.py:142
  13.4 0.9 %collective-permute-start.3 = (bf16[2,256,128]{2,1,0:T(8,128)(2,1)S(1)}, bf16[2,256,128]{2,1,0:T(8,128)(2,1)S(1)}, u32[]{:S(2)}, u32[]{:S(2)}) collective-permute-start(bf16[2,256,128]{2,1,0:T(8,128)(2,1)S(1)} %collective-permute-done.refs_4_), channel_id=1, source_target_pairs={{0,24},{8,16},{16,8},{24,0},{32,56},{40,48},{48,40},{56,32},{64,88... | collective-permute-start | bytes 393224 | tf_op jit(solution)/shard_map/ppermute | solution.py:142
  14.3 0.0 collective-permute-start.2
  14.3 1.4 %collective-permute-done.1.refs_5_ = bf16[2,256,128]{2,1,0:T(8,128)(2,1)S(1)} collective-permute-done((bf16[2,256,128]{2,1,0:T(8,128)(2,1)S(1)}, bf16[2,256,128]{2,1,0:T(8,128)(2,1)S(1)}, u32[]{:S(2)}, u32[]{:S(2)}) %collective-permute-start.1) | collective-permute-done | bytes 131104 | tf_op jit(solution)/shard_map/ppermute | solution.py:143
  15.7 0.0 copy-done.2
  15.7 0.0 copy-done.3
  15.7 2.8 %collective-permute-start.7 = (bf16[2,256,128]{2,1,0:T(8,128)(2,1)S(1)}, bf16[2,256,128]{2,1,0:T(8,128)(2,1)S(1)}, u32[]{:S(2)}, u32[]{:S(2)}) collective-permute-start(bf16[2,256,128]{2,1,0:T(8,128)(2,1)S(1)} %get-tuple-element.5), channel_id=1, source_target_pairs={{0,16},{8,24},{16,0},{24,8},{32,48},{40,56},{48,32},{56,40},{64,80... | collective-permute-start | bytes 393224 | tf_op jit(solution)/shard_map/ppermute | solution.py:146
  18.6 0.9 %collective-permute-start.6 = (bf16[2,256,128]{2,1,0:T(8,128)(2,1)S(1)}, bf16[2,256,128]{2,1,0:T(8,128)(2,1)S(1)}, u32[]{:S(2)}, u32[]{:S(2)}) collective-permute-start(bf16[2,256,128]{2,1,0:T(8,128)(2,1)S(1)} %get-tuple-element.6), channel_id=1, source_target_pairs={{0,24},{8,16},{16,8},{24,0},{32,56},{40,48},{48,40},{56,32},{64,88... | collective-permute-start | bytes 393224 | tf_op jit(solution)/shard_map/ppermute | solution.py:146
  19.4 0.0 collective-permute-done.4.refs_8_
  19.4 0.0 collective-permute-start.5
  19.4 0.0 collective-permute-done.3.refs_7_
  19.5 0.2 collective-permute-done.2.refs_6_
  19.6 2.2 %collective-permute-done.7.refs_11_ = bf16[2,256,128]{2,1,0:T(8,128)(2,1)S(1)} collective-permute-done((bf16[2,256,128]{2,1,0:T(8,128)(2,1)S(1)}, bf16[2,256,128]{2,1,0:T(8,128)(2,1)S(1)}, u32[]{:S(2)}, u32[]{:S(2)}) %collective-permute-start.7) | collective-permute-done | bytes 131104 | tf_op jit(solution)/shard_map/ppermute | solution.py:146
  21.9 3.1 %collective-permute-done.6.refs_10_ = bf16[2,256,128]{2,1,0:T(8,128)(2,1)S(1)} collective-permute-done((bf16[2,256,128]{2,1,0:T(8,128)(2,1)S(1)}, bf16[2,256,128]{2,1,0:T(8,128)(2,1)S(1)}, u32[]{:S(2)}, u32[]{:S(2)}) %collective-permute-start.6) | collective-permute-done | bytes 131104 | tf_op jit(solution)/shard_map/ppermute | solution.py:146
  25.0 0.0 collective-permute-done.5.refs_9_
  25.0 0.0 copy-done
  25.0 0.0 copy-done.1
  25.0 7.4 %attend.1 = bf16[256,1024]{1,0:T(8,128)(2,1)S(1)} custom-call(s32[16]{0:T(128)S(1)} %copy-done.1, s32[1]{0:T(128)} %bitcast.refs_1_, bf16[256,1024]{1,0:T(8,128)(2,1)S(1)} %copy-done, bf16[2,256,128]{2,1,0:T(8,128)(2,1)S(1)} %pad_maximum_fusion.refs_3_, bf16[2,256,128]{2,1,0:T(8,128)(2,1)S(1)} %collective-permute-done.refs_4_, ...), custom_call_target="tpu_custom_call" | custom-call | flops 4831838208 | bytes 1048576 | tf_op jit(solution)/shard_map/attend/pallas_call | solution.py:113
  32.4 16.0 %all_to_all.19 = bf16[8,32,1024]{2,1,0:T(8,128)(2,1)S(1)} all-to-all(bf16[8,32,1024]{2,1,0:T(8,128)(2,1)S(1)} %bitcast.7), channel_id=1, replica_groups=mesh['ctx'=32,'kvh'=8] {'kvh'}, dimensions={0} | all-to-all | bytes 1048576 | tf_op jit(solution)/shard_map/all_to_all | solution.py:153
  48.5 0.8 %copy.6 = bf16[8,4,8,1024]{3,2,0,1:T(8,128)(2,1)} copy(bf16[8,4,8,1024]{3,2,1,0:T(8,128)(2,1)S(1)} %bitcast.8) | data formatting | bytes 1048576 | tf_op jit(solution)/shard_map/all_to_all | solution.py:153
  (5 shorter events, 0.0 us)
Async XLA Ops:
  0.0 15.7 %copy-start.2 = (bf16[256,128]{1,0:T(8,128)(2,1)S(1)}, bf16[256,128]{1,0:T(8,128)(2,1)}, u32[]{:S(2)}) copy-start(bf16[256,128]{1,0:T(8,128)(2,1)} %param.6) | copy-start | bytes 196612
  0.0 15.7 %copy-start.3 = (bf16[256,128]{1,0:T(8,128)(2,1)S(1)}, bf16[256,128]{1,0:T(8,128)(2,1)}, u32[]{:S(2)}) copy-start(bf16[256,128]{1,0:T(8,128)(2,1)} %param.5) | copy-start | bytes 196612
  0.0 25.0 %copy-start = (bf16[256,1024]{1,0:T(8,128)(2,1)S(1)}, bf16[256,1024]{1,0:T(8,128)(2,1)}, u32[]{:S(2)}) copy-start(bf16[256,1024]{1,0:T(8,128)(2,1)} %refs_2_.1) | copy-start | bytes 1572868
  1.0 9.7 %collective-permute-start = (bf16[2,256,128]{2,1,0:T(8,128)(2,1)S(1)}, bf16[2,256,128]{2,1,0:T(8,128)(2,1)S(1)}, u32[]{:S(2)}, u32[]{:S(2)}) collective-permute-start(bf16[2,256,128]{2,1,0:T(8,128)(2,1)S(1)} %pad_maximum_fusion.refs_3_), channel_id=1, source_target_pairs={{0,32},{8,40},{16,48},{24,56},{32,64},{40,72},{48,80},{56,88},{64,... | collective-permute-start | bytes 393224 | tf_op jit(solution)/shard_map/ppermute | solution.py:141
  10.7 5.0 %collective-permute-start.1 = (bf16[2,256,128]{2,1,0:T(8,128)(2,1)S(1)}, bf16[2,256,128]{2,1,0:T(8,128)(2,1)S(1)}, u32[]{:S(2)}, u32[]{:S(2)}) collective-permute-start(bf16[2,256,128]{2,1,0:T(8,128)(2,1)S(1)} %collective-permute-done.refs_4_), channel_id=1, source_target_pairs={{0,32},{8,40},{16,48},{24,56},{32,64},{40,72},{48,80},{56,88},{64,... | collective-permute-start | bytes 393224 | tf_op jit(solution)/shard_map/ppermute | solution.py:143
  10.7 8.8 %collective-permute-start.4 = (bf16[2,256,128]{2,1,0:T(8,128)(2,1)S(1)}, bf16[2,256,128]{2,1,0:T(8,128)(2,1)S(1)}, u32[]{:S(2)}, u32[]{:S(2)}) collective-permute-start(bf16[2,256,128]{2,1,0:T(8,128)(2,1)S(1)} %collective-permute-done.refs_4_), channel_id=1, source_target_pairs={{0,16},{8,24},{16,0},{24,8},{32,48},{40,56},{48,32},{56,40},{64,80... | collective-permute-start | bytes 393224 | tf_op jit(solution)/shard_map/ppermute | solution.py:142
  13.4 6.0 %collective-permute-start.3 = (bf16[2,256,128]{2,1,0:T(8,128)(2,1)S(1)}, bf16[2,256,128]{2,1,0:T(8,128)(2,1)S(1)}, u32[]{:S(2)}, u32[]{:S(2)}) collective-permute-start(bf16[2,256,128]{2,1,0:T(8,128)(2,1)S(1)} %collective-permute-done.refs_4_), channel_id=1, source_target_pairs={{0,24},{8,16},{16,8},{24,0},{32,56},{40,48},{48,40},{56,32},{64,88... | collective-permute-start | bytes 393224 | tf_op jit(solution)/shard_map/ppermute | solution.py:142
  14.3 5.4 %collective-permute-start.2 = (bf16[2,256,128]{2,1,0:T(8,128)(2,1)S(1)}, bf16[2,256,128]{2,1,0:T(8,128)(2,1)S(1)}, u32[]{:S(2)}, u32[]{:S(2)}) collective-permute-start(bf16[2,256,128]{2,1,0:T(8,128)(2,1)S(1)} %collective-permute-done.refs_4_), channel_id=1, source_target_pairs={{0,8},{8,0},{16,24},{24,16},{32,40},{40,32},{48,56},{56,48},{64,72... | collective-permute-start | bytes 393224 | tf_op jit(solution)/shard_map/ppermute | solution.py:142
  15.7 6.1 %collective-permute-start.7 = (bf16[2,256,128]{2,1,0:T(8,128)(2,1)S(1)}, bf16[2,256,128]{2,1,0:T(8,128)(2,1)S(1)}, u32[]{:S(2)}, u32[]{:S(2)}) collective-permute-start(bf16[2,256,128]{2,1,0:T(8,128)(2,1)S(1)} %get-tuple-element.5), channel_id=1, source_target_pairs={{0,16},{8,24},{16,0},{24,8},{32,48},{40,56},{48,32},{56,40},{64,80... | collective-permute-start | bytes 393224 | tf_op jit(solution)/shard_map/ppermute | solution.py:146
  18.6 6.4 %collective-permute-start.6 = (bf16[2,256,128]{2,1,0:T(8,128)(2,1)S(1)}, bf16[2,256,128]{2,1,0:T(8,128)(2,1)S(1)}, u32[]{:S(2)}, u32[]{:S(2)}) collective-permute-start(bf16[2,256,128]{2,1,0:T(8,128)(2,1)S(1)} %get-tuple-element.6), channel_id=1, source_target_pairs={{0,24},{8,16},{16,8},{24,0},{32,56},{40,48},{48,40},{56,32},{64,88... | collective-permute-start | bytes 393224 | tf_op jit(solution)/shard_map/ppermute | solution.py:146
  19.4 5.6 %copy-start.1 = (s32[16]{0:T(128)S(1)}, s32[16]{0:T(128)}, u32[]{:S(2)}) copy-start(s32[16]{0:T(128)} %refs_0_.1) | copy-start | bytes 196
  19.4 5.6 %collective-permute-start.5 = (bf16[2,256,128]{2,1,0:T(8,128)(2,1)S(1)}, bf16[2,256,128]{2,1,0:T(8,128)(2,1)S(1)}, u32[]{:S(2)}, u32[]{:S(2)}) collective-permute-start(bf16[2,256,128]{2,1,0:T(8,128)(2,1)S(1)} %get-tuple-element.7), channel_id=1, source_target_pairs={{0,8},{8,0},{16,24},{24,16},{32,40},{40,32},{48,56},{56,48},{64,72... | collective-permute-start | bytes 393224 | tf_op jit(solution)/shard_map/ppermute | solution.py:146

commit v2 on v1

v2 whole, which is shorter than its diff:
```python
import functools

import jax
import jax.numpy as jnp
from jax import lax
from jax.experimental import pallas as pl
from jax.experimental.pallas import tpu as pltpu
from jax.sharding import PartitionSpec as P

HEADS = 8
DIM = 128
ROWS = 256
NDOCS = 16
NX = 4
NY = 4
SHARE = 32
BIG = float(2**18)
SCALE = 1.0 / DIM**0.5
F32 = jnp.float32
BF16 = jnp.bfloat16
VMEM = pl.BlockSpec(memory_space=pltpu.VMEM)
SMEM = pl.BlockSpec(memory_space=pltpu.SMEM)


def bounds(len_ref):
    lane = lax.broadcasted_iota(jnp.int32, (1, DIM), 1)
    first = jnp.full((1, DIM), 2**30, jnp.int32)
    last = jnp.full((1, DIM), 2**30, jnp.int32)
    first = jnp.where(lane == NDOCS, -(2**30), first)
    last = jnp.where(lane == NDOCS, 0, last)
    at = jnp.int32(0)
    for d in range(NDOCS):
        first = jnp.where(lane == d, at, first)
        at = at + len_ref[d]
        last = jnp.where(lane == d, at, last)
    return first, last


def own_row(r, y, core):
    return ((r & ~63) ^ (y << 6)) | ((r & 32) ^ (core << 5)) | (r & 31)


def block_of(kind, d, place, x):
    row = place - x
    if kind == "z":
        return place - NX * d
    if kind == "row":
        return row - NX + (x ^ d)
    other = x ^ d
    return jnp.where(other < x, row, row - 2 * NX) + other


def attend(kinds, lo, hi, opening, final, *refs):
    n = len(kinds)
    len_ref, place_ref = refs[:2]
    rest = list(refs[2:])
    place, y, core = place_ref[0], place_ref[1], place_ref[2]
    x = lax.rem(place, NX)
    q_ref = rest.pop(0)
    if not opening:
        qa_ref = rest.pop(0)
    kv = []
    while len(kv) < n:
        ref = rest.pop(0)
        if kinds[len(kv)] == ("either", 2):
            kv.append((ref, rest.pop(0)))
        elif len(ref.shape) == 4:
            kv += [ref.at[0], ref.at[1]]
        else:
            kv.append(ref)
    if not opening:
        state_in = rest[:3]
        rest = rest[3:]
    outs = rest[:-2]
    ka_ref, va_ref = rest[-2:]
    if not final:
        acc_out, tot_out, top_out = outs[:3]
        if opening:
            qp_ref, qa_ref = outs[3:]
    first, last = bounds(len_ref)
    if opening:
        for m in range(ROWS // SHARE):
            start = pl.multiple_of(own_row(m * SHARE, y, core), SHARE)
            qp_ref[m * SHARE : (m + 1) * SHARE, :] = q_ref[pl.ds(start, SHARE), :]
        pos = place * ROWS + own_row(lax.broadcasted_iota(jnp.int32, (ROWS, DIM), 0), y, core)
        qa_ref[...] = jnp.where((pos >= first) & (pos < last), 0.0, -BIG).astype(BF16)
        q_ref = qp_ref
    for b, (kind, d) in enumerate(kinds):
        rows = slice(b * ROWS, (b + 1) * ROWS)
        if kind == "either":
            late = x < (x ^ d)
            key = jnp.where(late, kv[b][1][0], kv[b][0][0])
            val = jnp.where(late, kv[b][1][1], kv[b][0][1])
        else:
            key, val = kv[b][0], kv[b][1]
        pos = block_of(kind, d, place, x) * ROWS + lax.broadcasted_iota(jnp.int32, (ROWS, DIM), 0)
        ka_ref[rows, :DIM] = key
        ka_ref[rows, DIM:] = jnp.where((pos >= first) & (pos < last), 1.0, 0.0).astype(BF16)
        va_ref[rows, :DIM] = val
        va_ref[rows, DIM:] = jnp.ones((ROWS, DIM), BF16)
    many = hi - lo
    for h in range(HEADS):
        cols = slice(h * DIM, (h + 1) * DIM)
        qq = jnp.concatenate([q_ref[lo:hi, cols], qa_ref[lo:hi, :]], axis=1)
        s = lax.dot_general(qq, ka_ref[...], (((1,), (1,)), ((), ())), preferred_element_type=F32)
        parts = []
        for b, (kind, d) in enumerate(kinds):
            c = s[:, b * ROWS : (b + 1) * ROWS]
            if (kind, d) == ("z", 0):
                r_id = own_row(lax.broadcasted_iota(jnp.int32, (many, ROWS), 0) + lo, y, core)
                c_id = lax.broadcasted_iota(jnp.int32, (many, ROWS), 1)
                c = jnp.where(c_id <= r_id, c, -BIG)
            parts += [c[:, :DIM], c[:, DIM:]]
        top = parts[0]
        for c in parts[1:]:
            top = jnp.maximum(top, c)
        top = jnp.broadcast_to(jnp.max(top, axis=1, keepdims=True), (many, DIM))
        if not opening:
            old = state_in[2][h, lo:hi, :]
            top = jnp.maximum(old, top)
            keep = jnp.exp((old - top) * SCALE)
        p = jnp.concatenate([jnp.exp((c - top) * SCALE).astype(BF16) for c in parts], axis=1)
        mixed = jnp.dot(p, va_ref[...], preferred_element_type=F32)
        acc, tot = mixed[:, :DIM], mixed[:, DIM:]
        if not opening:
            acc = acc + state_in[0][h, lo:hi, :] * keep
            tot = tot + state_in[1][h, lo:hi, :] * keep
        if final:
            res = (acc / tot).astype(BF16)
            for i, out in enumerate(outs):
                out[:, cols] = res[i * 2 * SHARE : (i + 1) * 2 * SHARE, :]
        else:
            acc_out[h] = acc
            tot_out[h] = tot
            top_out[h] = top


def attend_part(lengths, place, q, parts, state=None, final=False, lo=0, hi=ROWS):
    kinds = tuple(k for ks, _ in parts for k in ks)
    n = len(kinds)
    opening = state is None
    arrays = list(q)
    for _, a in parts:
        arrays += list(a) if isinstance(a, tuple) else [a]
    arrays += list(state or ())
    part = jax.ShapeDtypeStruct((HEADS, ROWS, DIM), F32)
    if final:
        outs = [jax.ShapeDtypeStruct((2 * SHARE, HEADS * DIM), BF16)] * ((hi - lo) // (2 * SHARE))
    else:
        outs = [part] * 3
        if opening:
            outs += [jax.ShapeDtypeStruct((ROWS, HEADS * DIM), BF16), jax.ShapeDtypeStruct((ROWS, DIM), BF16)]
    return pl.pallas_call(
        functools.partial(attend, kinds, lo, hi, opening, final),
        out_shape=outs,
        in_specs=[SMEM, SMEM] + [VMEM] * len(arrays),
        out_specs=[VMEM] * len(outs),
        scratch_shapes=[pltpu.VMEM((n * ROWS, 2 * DIM), BF16)] * 2,
        cost_estimate=pl.CostEstimate(
            flops=8 * HEADS * (hi - lo) * ROWS * DIM * n,
            bytes_accessed=1 << 20,
            transcendentals=HEADS * (hi - lo) * ROWS * n,
        ),
        compiler_params=pltpu.CompilerParams(vmem_limit_bytes=40 * 2**20),
        name="attend",
    )(lengths, place, *arrays)


def lay_out(place_ref, *refs):
    y, core = place_ref[1], place_ref[2]
    pieces, got, out, sems = refs[:NY], refs[NY], refs[NY + 1], refs[NY + 2]
    width = HEADS * DIM
    copies = []
    for d in range(NY):
        for k in range(2):
            src = got.at[d] if k else pieces[d].at[pl.ds(0, SHARE), :]
            at = pl.multiple_of((((y ^ d) << 1) + (core ^ k)) * width, width)
            copies.append(pltpu.make_async_copy(src, out.at[:, pl.ds(at, width)], sems.at[2 * d + k]))
    for c in copies:
        c.start()
    for c in copies:
        c.wait()


def exchange(place, pieces):
    size = lax.axis_size("kvh")
    flip = lambda m: [(i, i ^ m) for i in range(size)]
    held = {0: pieces[0]}
    for d in (2, 1, 3):
        held[d] = lax.ppermute(pieces[d], "kvh", flip(2 * d))
    held = [held[d] for d in range(NY)]
    got = lax.ppermute(jnp.stack([h[SHARE:] for h in held]), "kvh", flip(1))
    anywhere = pl.BlockSpec(memory_space=pl.ANY)
    return pl.pallas_call(
        lay_out,
        out_shape=jax.ShapeDtypeStruct((SHARE, size * HEADS * DIM), BF16),
        in_specs=[SMEM] + [VMEM] * (NY + 1),
        out_specs=anywhere,
        scratch_shapes=[pltpu.SemaphoreType.DMA((2 * NY,))],
        compiler_params=pltpu.CompilerParams(vmem_limit_bytes=40 * 2**20),
        name="lay_out",
    )(place, *held, got)


def per_device(queries, keys, values, doc_lengths):
    size = lax.axis_size("ctx")
    down = [(i, (i + NX) % size) for i in range(size)]
    flip = lambda d: [(i, i ^ d) for i in range(size)]
    place = lax.axis_index("ctx")
    kvh = lax.axis_index("kvh")
    x = place % NX
    where = jnp.stack([place, kvh // 2, kvh % 2]).astype(jnp.int32)
    send = functools.partial(lax.ppermute, axis_name="ctx")
    own = jnp.stack([keys, values])
    one = send(own, perm=down)
    across = send(own, perm=flip(2))
    two = send(one, perm=down)
    one_across = send(across, perm=down)
    low = jnp.stack([one, jnp.where(x & 1 == 0, own, two)])
    high = jnp.stack([one, jnp.where(x & 2 == 0, own, two)])
    near = send(low, perm=flip(1))
    far = send(high, perm=flip(3))
    two_across = send(one_across, perm=down)
    p_own = ((("z", 0),), own)
    p_one = ((("z", 1),), one)
    p_two = ((("z", 2),), two)
    p_across = ((("row", 2),), one_across)
    p_near = ((("row", 1), ("mix", 1)), near)
    p_far = ((("row", 3), ("mix", 3)), far)
    p_either = ((("either", 2),), (across, two_across))
    groups = [[p_own, p_one], [p_two, p_across], [p_near, p_far, p_either]]
    *state, qp, qa = attend_part(doc_lengths, where, (queries,), groups[0])
    for g in groups[1:-1]:
        state = attend_part(doc_lengths, where, (qp, qa), g, state)
    pieces = attend_part(doc_lengths, where, (qp, qa), groups[-1], state, True)
    return exchange(where, pieces)


def solution(mesh):
    in_specs = (P("ctx", "kvh"), P("ctx", "kvh"), P("ctx", "kvh"), P())
    out_specs = P(("ctx", "kvh"), None)
    return jax.shard_map(
        per_device, mesh=mesh, in_specs=in_specs, out_specs=out_specs, check_vma=False
    )
```

time: 49.4 us -> 46.9 us (0.949)
  blocking collectives: 16 us -> 0 us
  starting transfers between devices: 9.85 us -> 18.3 us
  Pallas kernels: 7.41 us -> 11.4 us
  waiting for transfers between devices: 14.1 us -> 15.2 us
    all_to_all x1 -> x0, blocking collectives: 16 us -> none  [per_device(): lax.all_to_all(attended, 'kvh', split_axis=0, concat_axis=1, tiled=True)]
    ppermute x8 -> x11, starting transfers between devices: 9.85 us -> 18.3 us  [the longest x1 6.19 us: exchange(): got = lax.ppermute(jnp.stack([h[SHARE:] for h in held]), 'kvh', flip(1))]
    pallas_call x1 -> x4, Pallas kernels: 7.41 us -> 11.4 us  [the longest x3 10 us: attend_part(): pl.pallas_call(functools.partial(attend, kinds, lo, hi, opening, final),...]
    ppermute x8 -> x11, waiting for transfers between devices: 14.1 us -> 15.2 us  [the longest x1 5.01 us: per_device(): two = send(one, perm=down)]
    all_to_all x1 -> x0, local copies, waits for them, and re-layouts: 0.83 us -> none  [per_device(): lax.all_to_all(attended, 'kvh', split_axis=0, concat_axis=1, tiled=True)]
  transfers between devices with their start and end apart: 8 -> 11, of which waited for: 5 -> 5; matrix products, arithmetic and copies ran while one was open for 0% -> 0% of each run, Pallas kernels for 0% -> 11%
where the time goes in v2:
time: 46.9 us; the launch traced here: 46.7 us
  starting transfers between devices  18.3 us (39%)
  waiting for transfers between devices  15.2 us (32%)
  Pallas kernels  11.4 us (24%)
  other arithmetic  1.1 us (2%)
    pallas_call x3, Pallas kernels, attend_part(): pl.pallas_call(functools.partial(attend, kinds, lo, hi, opening, final),...  10 us
    ppermute x1, starting transfers between devices, exchange(): got = lax.ppermute(jnp.stack([h[SHARE:] for h in held]), 'kvh', flip(1))  6.19 us
    ppermute x1, waiting for transfers between devices, per_device(): two = send(one, perm=down)  5.01 us
    ppermute x3, waiting for transfers between devices, exchange(): held[d] = lax.ppermute(pieces[d], 'kvh', flip(2 * d))  4.63 us
    ppermute x1, waiting for transfers between devices, per_device(): one = send(own, perm=down)  4.42 us
    ppermute x3, starting transfers between devices, exchange(): held[d] = lax.ppermute(pieces[d], 'kvh', flip(2 * d))  3.5 us
    ppermute x1, starting transfers between devices, per_device(): across = send(own, perm=flip(2))  2.74 us
    ppermute x1, starting transfers between devices, per_device(): one = send(own, perm=down)  2.54 us
  transfers between devices with their start and end apart: 11, of which 5 were waited for; matrix products, arithmetic and copies ran while one was open for 0% of the time, Pallas kernels for 11%

profile of v2, /device:TPU:1, one launch (start us, length us, event | category | flops | bytes accessed | tf_op | source)
XLA Modules:
  0.0 46.7 jit_solution(3357592633918659696)
XLA Ops:
  0.0 0.9 %pad_maximum_fusion.3.refs_3_ = bf16[2,256,128]{2,1,0:T(8,128)(2,1)S(1)} fusion(bf16[1,256,128]{2,1,0:T(8,128)(2,1)} %bitcast.19, bf16[1,256,128]{2,1,0:T(8,128)(2,1)} %bitcast.21), kind=kLoop, calls=%fused_computation.3 | loop fusion | flops 65536 | bytes 262144 | tf_op jit(solution)/shard_map/stack | solution.py:214
  0.9 0.0 copy-start.2
  0.9 2.5 %collective-permute-start = (bf16[2,256,128]{2,1,0:T(8,128)(2,1)S(1)}, bf16[2,256,128]{2,1,0:T(8,128)(2,1)S(1)}, u32[]{:S(2)}, u32[]{:S(2)}) collective-permute-start(bf16[2,256,128]{2,1,0:T(8,128)(2,1)S(1)} %pad_maximum_fusion.3.refs_3_), channel_id=1, source_target_pairs={{0,32},{8,40},{16,48},{24,56},{32,64},{40,72},{48,80},{56,88},{64,... | collective-permute-start | bytes 393224 | tf_op jit(solution)/shard_map/ppermute | solution.py:215
  3.5 2.7 %collective-permute-start.4 = (bf16[2,256,128]{2,1,0:T(8,128)(2,1)S(1)}, bf16[2,256,128]{2,1,0:T(8,128)(2,1)S(1)}, u32[]{:S(2)}, u32[]{:S(2)}) collective-permute-start(bf16[2,256,128]{2,1,0:T(8,128)(2,1)S(1)} %pad_maximum_fusion.3.refs_3_), channel_id=1, source_target_pairs={{0,16},{8,24},{16,0},{24,8},{32,48},{40,56},{48,32},{56,40},{64,80... | collective-permute-start | bytes 393224 | tf_op jit(solution)/shard_map/ppermute | solution.py:216
  6.2 4.4 %collective-permute-done.refs_4_ = bf16[2,256,128]{2,1,0:T(8,128)(2,1)S(1)} collective-permute-done((bf16[2,256,128]{2,1,0:T(8,128)(2,1)S(1)}, bf16[2,256,128]{2,1,0:T(8,128)(2,1)S(1)}, u32[]{:S(2)}, u32[]{:S(2)}) %collective-permute-start) | collective-permute-done | bytes 131104 | tf_op jit(solution)/shard_map/ppermute | solution.py:215
  10.6 0.0 collective-permute-start.1
  10.7 5.0 %collective-permute-done.1.refs_4_ = bf16[2,256,128]{2,1,0:T(8,128)(2,1)S(1)} collective-permute-done((bf16[2,256,128]{2,1,0:T(8,128)(2,1)S(1)}, bf16[2,256,128]{2,1,0:T(8,128)(2,1)S(1)}, u32[]{:S(2)}, u32[]{:S(2)}) %collective-permute-start.1) | collective-permute-done | bytes 131104 | tf_op jit(solution)/shard_map/ppermute | solution.py:217
  15.7 0.0 copy-start.1
  15.8 1.3 %collective-permute-start.2 = (bf16[2,2,256,128]{3,2,1,0:T(8,128)(2,1)S(1)}, bf16[2,2,256,128]{3,2,1,0:T(8,128)(2,1)S(1)}, u32[]{:S(2)}, u32[]{:S(2)}) collective-permute-start(bf16[2,2,256,128]{3,2,1,0:T(8,128)(2,1)S(1)} %get-tuple-element.32), channel_id=1, source_target_pairs={{0,8},{8,0},{16,24},{24,16},{32,40},{40,32},{48,56},{56,48},{64,72... | collective-permute-start | bytes 786440 | tf_op jit(solution)/shard_map/ppermute | solution.py:221
  17.1 1.8 %collective-permute-start.3 = (bf16[2,2,256,128]{3,2,1,0:T(8,128)(2,1)S(1)}, bf16[2,2,256,128]{3,2,1,0:T(8,128)(2,1)S(1)}, u32[]{:S(2)}, u32[]{:S(2)}) collective-permute-start(bf16[2,2,256,128]{3,2,1,0:T(8,128)(2,1)S(1)} %get-tuple-element.31), channel_id=1, source_target_pairs={{0,24},{8,16},{16,8},{24,0},{32,56},{40,48},{48,40},{56,32},{64,88... | collective-permute-start | bytes 786440 | tf_op jit(solution)/shard_map/ppermute | solution.py:222
  18.9 0.1 pad_add_fusion.refs_1_.place_ref
  19.0 0.2 collective-permute-start.6
  19.2 0.3 copy-done
  19.5 2.5 %attend.3 = (f32[8,256,128]{2,1,0:T(8,128)S(1)}, f32[8,256,128]{2,1,0:T(8,128)S(1)}, f32[8,256,128]{2,1,0:T(8,128)S(1)}, bf16[256,1024]{1,0:T(8,128)(2,1)S(1)}, bf16[256,128]{1,0:T(8,128)(2,1)S(1)}) custom-call(s32[16]{0:T(128)S(1)} %copy-done, s32[3]{0:T(128)S(1)} %pad_add_fusion.refs_1_.place_ref, bf16[256,1024]{1,0:T(8,128)(2,1)S(1)} %copy-done.1, ...), custom_call_target="tpu_custom_call" | custom-call | flops 1073741824 | bytes 1048576 | tf_op jit(solution)/shard_map/attend/pallas_call | solution.py:153
  22.0 2.7 %attend.4 = (f32[8,256,128]{2,1,0:T(8,128)S(1)}, f32[8,256,128]{2,1,0:T(8,128)S(1)}, f32[8,256,128]{2,1,0:T(8,128)S(1)}) custom-call(s32[16]{0:T(128)S(1)} %copy-done, s32[3]{0:T(128)S(1)} %pad_add_fusion.refs_1_.place_ref, bf16[256,1024]{1,0:T(8,128)(2,1)S(1)} %get-tuple-element.17.refs_2_, bf16[256,128]{1,0:T(8,128)(2,1)S(1)} %get-tuple-element.18.refs_3_, ...), custom_call_target="tpu_custom_call" | custom-call | flops 1073741824 | bytes 1048576 | tf_op jit(solution)/shard_map/attend/pallas_call | solution.py:153
  24.7 4.9 %attend.5 = (bf16[64,1024]{1,0:T(8,128)(2,1)S(1)}, bf16[64,1024]{1,0:T(8,128)(2,1)S(1)}, bf16[64,1024]{1,0:T(8,128)(2,1)S(1)}, bf16[64,1024]{1,0:T(8,128)(2,1)S(1)}) custom-call(s32[16]{0:T(128)S(1)} %copy-done, s32[3]{0:T(128)S(1)} %pad_add_fusion.refs_1_.place_ref, bf16[256,1024]{1,0:T(8,128)(2,1)S(1)} %get-tuple-element.17.refs_2_, ...), custom_call_target="tpu_custom_call" | custom-call | flops 2684354560 | bytes 1048576 | tf_op jit(solution)/shard_map/attend/pallas_call | solution.py:153
  29.6 2.8 %collective-permute-start.9 = (bf16[64,1024]{1,0:T(8,128)(2,1)S(1)}, bf16[64,1024]{1,0:T(8,128)(2,1)S(1)}, u32[]{:S(2)}, u32[]{:S(2)}) collective-permute-start(bf16[64,1024]{1,0:T(8,128)(2,1)S(1)} %get-tuple-element.28), channel_id=1, source_target_pairs={{0,6},{1,7},{2,4},{3,5},{4,2},{5,3},{6,0},{7,1},{8,14},{9,15},{10,... | collective-permute-start | bytes 393224 | tf_op jit(solution)/shard_map/ppermute | solution.py:190
  32.4 0.3 collective-permute-start.8
  32.8 0.3 collective-permute-start.7
  33.1 2.6 %collective-permute-done.9.refs_3_ = bf16[64,1024]{1,0:T(8,128)(2,1)S(1)} collective-permute-done((bf16[64,1024]{1,0:T(8,128)(2,1)S(1)}, bf16[64,1024]{1,0:T(8,128)(2,1)S(1)}, u32[]{:S(2)}, u32[]{:S(2)}) %collective-permute-start.9) | collective-permute-done | bytes 131104 | tf_op jit(solution)/shard_map/ppermute | solution.py:190
  35.7 2.0 %collective-permute-done.8.refs_2_ = bf16[64,1024]{1,0:T(8,128)(2,1)S(1)} collective-permute-done((bf16[64,1024]{1,0:T(8,128)(2,1)S(1)}, bf16[64,1024]{1,0:T(8,128)(2,1)S(1)}, u32[]{:S(2)}, u32[]{:S(2)}) %collective-permute-start.8) | collective-permute-done | bytes 131104 | tf_op jit(solution)/shard_map/ppermute | solution.py:190
  37.8 6.2 %collective-permute-start.10 = (bf16[4,32,1024]{2,1,0:T(8,128)(2,1)S(1)}, bf16[4,32,1024]{2,1,0:T(8,128)(2,1)S(1)}, u32[]{:S(2)}, u32[]{:S(2)}) collective-permute-start(bf16[4,32,1024]{2,1,0:T(8,128)(2,1)S(1)} %pad_maximum_fusion.2), channel_id=1, source_target_pairs={{0,1},{1,0},{2,3},{3,2},{4,5},{5,4},{6,7},{7,6},{8,9},{9,8},{10,11... | collective-permute-start | bytes 786440 | tf_op jit(solution)/shard_map/ppermute | solution.py:192
  44.0 1.2 %collective-permute-done.10.refs_4_ = bf16[4,32,1024]{2,1,0:T(8,128)(2,1)S(1)} collective-permute-done((bf16[4,32,1024]{2,1,0:T(8,128)(2,1)S(1)}, bf16[4,32,1024]{2,1,0:T(8,128)(2,1)S(1)}, u32[]{:S(2)}, u32[]{:S(2)}) %collective-permute-start.10) | collective-permute-done | bytes 262176 | tf_op jit(solution)/shard_map/ppermute | solution.py:192
  45.2 1.4 %lay_out.1 = bf16[32,8192]{1,0:T(8,128)(2,1)} custom-call(s32[3]{0:T(128)S(1)} %pad_add_fusion.refs_1_.place_ref, bf16[64,1024]{1,0:T(8,128)(2,1)S(1)} %get-tuple-element.25.refs_0_, bf16[64,1024]{1,0:T(8,128)(2,1)S(1)} %collective-permute-done.7.refs_1_, bf16[64,1024]{1,0:T(8,128)(2,1)S(1)} %collective-permute-done.8.refs_2_, ...), custom_call_target="tpu_custom_call" | custom-call | tf_op jit(solution)/shard_map/lay_out/pallas_call | solution.py:194
  (19 shorter events, 0.2 us)
Async XLA Ops:
  0.0 15.7 %copy-start.3 = (bf16[256,128]{1,0:T(8,128)(2,1)S(1)}, bf16[256,128]{1,0:T(8,128)(2,1)}, u32[]{:S(2)}) copy-start(bf16[256,128]{1,0:T(8,128)(2,1)} %param.5) | copy-start | bytes 196612
  0.9 14.8 %copy-start.2 = (bf16[256,128]{1,0:T(8,128)(2,1)S(1)}, bf16[256,128]{1,0:T(8,128)(2,1)}, u32[]{:S(2)}) copy-start(bf16[256,128]{1,0:T(8,128)(2,1)} %param.6) | copy-start | bytes 196612
  0.9 9.7 %collective-permute-start = (bf16[2,256,128]{2,1,0:T(8,128)(2,1)S(1)}, bf16[2,256,128]{2,1,0:T(8,128)(2,1)S(1)}, u32[]{:S(2)}, u32[]{:S(2)}) collective-permute-start(bf16[2,256,128]{2,1,0:T(8,128)(2,1)S(1)} %pad_maximum_fusion.3.refs_3_), channel_id=1, source_target_pairs={{0,32},{8,40},{16,48},{24,56},{32,64},{40,72},{48,80},{56,88},{64,... | collective-permute-start | bytes 393224 | tf_op jit(solution)/shard_map/ppermute | solution.py:215
  3.5 7.2 %collective-permute-start.4 = (bf16[2,256,128]{2,1,0:T(8,128)(2,1)S(1)}, bf16[2,256,128]{2,1,0:T(8,128)(2,1)S(1)}, u32[]{:S(2)}, u32[]{:S(2)}) collective-permute-start(bf16[2,256,128]{2,1,0:T(8,128)(2,1)S(1)} %pad_maximum_fusion.3.refs_3_), channel_id=1, source_target_pairs={{0,16},{8,24},{16,0},{24,8},{32,48},{40,56},{48,32},{56,40},{64,80... | collective-permute-start | bytes 393224 | tf_op jit(solution)/shard_map/ppermute | solution.py:216
  10.6 5.0 %collective-permute-start.1 = (bf16[2,256,128]{2,1,0:T(8,128)(2,1)S(1)}, bf16[2,256,128]{2,1,0:T(8,128)(2,1)S(1)}, u32[]{:S(2)}, u32[]{:S(2)}) collective-permute-start(bf16[2,256,128]{2,1,0:T(8,128)(2,1)S(1)} %collective-permute-done.refs_4_), channel_id=1, source_target_pairs={{0,32},{8,40},{16,48},{24,56},{32,64},{40,72},{48,80},{56,88},{64,... | collective-permute-start | bytes 393224 | tf_op jit(solution)/shard_map/ppermute | solution.py:217
  10.7 8.3 %collective-permute-start.5 = (bf16[2,256,128]{2,1,0:T(8,128)(2,1)S(1)}, bf16[2,256,128]{2,1,0:T(8,128)(2,1)S(1)}, u32[]{:S(2)}, u32[]{:S(2)}) collective-permute-start(bf16[2,256,128]{2,1,0:T(8,128)(2,1)S(1)} %collective-permute-done.4.refs_6_), channel_id=1, source_target_pairs={{0,32},{8,40},{16,48},{24,56},{32,64},{40,72},{48,80},{56,88},{64,... | collective-permute-start | bytes 393224 | tf_op jit(solution)/shard_map/ppermute | solution.py:218
  15.7 3.5 %copy-start.1 = (bf16[256,1024]{1,0:T(8,128)(2,1)S(1)}, bf16[256,1024]{1,0:T(8,128)(2,1)}, u32[]{:S(2)}) copy-start(bf16[256,1024]{1,0:T(8,128)(2,1)} %refs_2_.1) | copy-start | bytes 1572868
  15.8 8.9 %collective-permute-start.2 = (bf16[2,2,256,128]{3,2,1,0:T(8,128)(2,1)S(1)}, bf16[2,2,256,128]{3,2,1,0:T(8,128)(2,1)S(1)}, u32[]{:S(2)}, u32[]{:S(2)}) collective-permute-start(bf16[2,2,256,128]{3,2,1,0:T(8,128)(2,1)S(1)} %get-tuple-element.32), channel_id=1, source_target_pairs={{0,8},{8,0},{16,24},{24,16},{32,40},{40,32},{48,56},{56,48},{64,72... | collective-permute-start | bytes 786440 | tf_op jit(solution)/shard_map/ppermute | solution.py:221
  17.1 7.7 %collective-permute-start.3 = (bf16[2,2,256,128]{3,2,1,0:T(8,128)(2,1)S(1)}, bf16[2,2,256,128]{3,2,1,0:T(8,128)(2,1)S(1)}, u32[]{:S(2)}, u32[]{:S(2)}) collective-permute-start(bf16[2,2,256,128]{3,2,1,0:T(8,128)(2,1)S(1)} %get-tuple-element.31), channel_id=1, source_target_pairs={{0,24},{8,16},{16,8},{24,0},{32,56},{40,48},{48,40},{56,32},{64,88... | collective-permute-start | bytes 786440 | tf_op jit(solution)/shard_map/ppermute | solution.py:222
  18.9 0.7 %copy-start = (s32[16]{0:T(128)S(1)}, s32[16]{0:T(128)}, u32[]{:S(2)}) copy-start(s32[16]{0:T(128)} %refs_0_.5) | copy-start | bytes 196
  19.0 5.7 %collective-permute-start.6 = (bf16[2,256,128]{2,1,0:T(8,128)(2,1)S(1)}, bf16[2,256,128]{2,1,0:T(8,128)(2,1)S(1)}, u32[]{:S(2)}, u32[]{:S(2)}) collective-permute-start(bf16[2,256,128]{2,1,0:T(8,128)(2,1)S(1)} %collective-permute-done.5.refs_5_), channel_id=1, source_target_pairs={{0,32},{8,40},{16,48},{24,56},{32,64},{40,72},{48,80},{56,88},{64,... | collective-permute-start | bytes 393224 | tf_op jit(solution)/shard_map/ppermute | solution.py:223
  29.6 6.1 %collective-permute-start.9 = (bf16[64,1024]{1,0:T(8,128)(2,1)S(1)}, bf16[64,1024]{1,0:T(8,128)(2,1)S(1)}, u32[]{:S(2)}, u32[]{:S(2)}) collective-permute-start(bf16[64,1024]{1,0:T(8,128)(2,1)S(1)} %get-tuple-element.28), channel_id=1, source_target_pairs={{0,6},{1,7},{2,4},{3,5},{4,2},{5,3},{6,0},{7,1},{8,14},{9,15},{10,... | collective-permute-start | bytes 393224 | tf_op jit(solution)/shard_map/ppermute | solution.py:190
  32.4 5.3 %collective-permute-start.8 = (bf16[64,1024]{1,0:T(8,128)(2,1)S(1)}, bf16[64,1024]{1,0:T(8,128)(2,1)S(1)}, u32[]{:S(2)}, u32[]{:S(2)}) collective-permute-start(bf16[64,1024]{1,0:T(8,128)(2,1)S(1)} %get-tuple-element.27), channel_id=1, source_target_pairs={{0,4},{1,5},{2,6},{3,7},{4,0},{5,1},{6,2},{7,3},{8,12},{9,13},{10,... | collective-permute-start | bytes 393224 | tf_op jit(solution)/shard_map/ppermute | solution.py:190
  32.8 5.0 %collective-permute-start.7 = (bf16[64,1024]{1,0:T(8,128)(2,1)S(1)}, bf16[64,1024]{1,0:T(8,128)(2,1)S(1)}, u32[]{:S(2)}, u32[]{:S(2)}) collective-permute-start(bf16[64,1024]{1,0:T(8,128)(2,1)S(1)} %get-tuple-element.26), channel_id=1, source_target_pairs={{0,2},{1,3},{2,0},{3,1},{4,6},{5,7},{6,4},{7,5},{8,10},{9,11},{10,... | collective-permute-start | bytes 393224 | tf_op jit(solution)/shard_map/ppermute | solution.py:190
  37.8 7.4 %collective-permute-start.10 = (bf16[4,32,1024]{2,1,0:T(8,128)(2,1)S(1)}, bf16[4,32,1024]{2,1,0:T(8,128)(2,1)S(1)}, u32[]{:S(2)}, u32[]{:S(2)}) collective-permute-start(bf16[4,32,1024]{2,1,0:T(8,128)(2,1)S(1)} %pad_maximum_fusion.2), channel_id=1, source_target_pairs={{0,1},{1,0},{2,3},{3,2},{4,5},{5,4},{6,7},{7,6},{8,9},{9,8},{10,11... | collective-permute-start | bytes 786440 | tf_op jit(solution)/shard_map/ppermute | solution.py:192

commit v3 on v2

--- a/solution.py
+++ b/solution.py
@@ -1,4 +1,5 @@
 import functools
+import math
 
 import jax
 import jax.numpy as jnp
@@ -15,7 +16,7 @@
 NY = 4
 SHARE = 32
 BIG = float(2**18)
-SCALE = 1.0 / DIM**0.5
+SCALE = math.log2(math.e) / DIM**0.5
 F32 = jnp.float32
 BF16 = jnp.bfloat16
 VMEM = pl.BlockSpec(memory_space=pltpu.VMEM)
@@ -36,6 +37,15 @@
     return first, last
 
 
+def reach(len_ref, place):
+    at = jnp.int32(0)
+    begin = jnp.int32(0)
+    for d in range(NDOCS):
+        begin = jnp.where(at <= place * ROWS, at, begin)
+        at = at + len_ref[d]
+    return begin
+
+
 def own_row(r, y, core):
     return ((r & ~63) ^ (y << 6)) | ((r & 32) ^ (core << 5)) | (r & 31)
 
@@ -50,7 +60,7 @@
     return jnp.where(other < x, row, row - 2 * NX) + other
 
 
-def attend(kinds, lo, hi, opening, final, *refs):
+def attend(kinds, opening, final, *refs):
     n = len(kinds)
     len_ref, place_ref = refs[:2]
     rest = list(refs[2:])
@@ -85,57 +95,87 @@
         pos = place * ROWS + own_row(lax.broadcasted_iota(jnp.int32, (ROWS, DIM), 0), y, core)
         qa_ref[...] = jnp.where((pos >= first) & (pos < last), 0.0, -BIG).astype(BF16)
         q_ref = qp_ref
+    front, back = jnp.int32(0), jnp.int32(n - 1)
+    begin = reach(len_ref, place)
     for b, (kind, d) in enumerate(kinds):
-        rows = slice(b * ROWS, (b + 1) * ROWS)
         if kind == "either":
             late = x < (x ^ d)
             key = jnp.where(late, kv[b][1][0], kv[b][0][0])
             val = jnp.where(late, kv[b][1][1], kv[b][0][1])
         else:
             key, val = kv[b][0], kv[b][1]
-        pos = block_of(kind, d, place, x) * ROWS + lax.broadcasted_iota(jnp.int32, (ROWS, DIM), 0)
-        ka_ref[rows, :DIM] = key
-        ka_ref[rows, DIM:] = jnp.where((pos >= first) & (pos < last), 1.0, 0.0).astype(BF16)
-        va_ref[rows, :DIM] = val
+        start = block_of(kind, d, place, x) * ROWS
+        rows = slice(b * ROWS, (b + 1) * ROWS)
+        at = rows
+        if final:
+            used = (start + ROWS > begin).astype(jnp.int32)
+            at = pl.ds(pl.multiple_of(jnp.where(used == 1, front, back) * ROWS, ROWS), ROWS)
+            front, back = front + used, back - (1 - used)
+        pos = start + lax.broadcasted_iota(jnp.int32, (ROWS, DIM), 0)
+        ka_ref[:DIM, at] = key.T
+        ka_ref[DIM:, at] = jnp.where((pos >= first) & (pos < last), 1.0, 0.0).astype(BF16).T
+        va_ref[at, :DIM] = val
         va_ref[rows, DIM:] = jnp.ones((ROWS, DIM), BF16)
-    many = hi - lo
-    for h in range(HEADS):
-        cols = slice(h * DIM, (h + 1) * DIM)
-        qq = jnp.concatenate([q_ref[lo:hi, cols], qa_ref[lo:hi, :]], axis=1)
-        s = lax.dot_general(qq, ka_ref[...], (((1,), (1,)), ((), ())), preferred_element_type=F32)
-        parts = []
-        for b, (kind, d) in enumerate(kinds):
-            c = s[:, b * ROWS : (b + 1) * ROWS]
-            if (kind, d) == ("z", 0):
-                r_id = own_row(lax.broadcasted_iota(jnp.int32, (many, ROWS), 0) + lo, y, core)
-                c_id = lax.broadcasted_iota(jnp.int32, (many, ROWS), 1)
-                c = jnp.where(c_id <= r_id, c, -BIG)
-            parts += [c[:, :DIM], c[:, DIM:]]
-        top = parts[0]
-        for c in parts[1:]:
-            top = jnp.maximum(top, c)
-        top = jnp.broadcast_to(jnp.max(top, axis=1, keepdims=True), (many, DIM))
-        if not opening:
-            old = state_in[2][h, lo:hi, :]
-            top = jnp.maximum(old, top)
-            keep = jnp.exp((old - top) * SCALE)
-        p = jnp.concatenate([jnp.exp((c - top) * SCALE).astype(BF16) for c in parts], axis=1)
-        mixed = jnp.dot(p, va_ref[...], preferred_element_type=F32)
-        acc, tot = mixed[:, :DIM], mixed[:, DIM:]
-        if not opening:
-            acc = acc + state_in[0][h, lo:hi, :] * keep
-            tot = tot + state_in[1][h, lo:hi, :] * keep
-        if final:
-            res = (acc / tot).astype(BF16)
-            for i, out in enumerate(outs):
-                out[:, cols] = res[i * 2 * SHARE : (i + 1) * 2 * SHARE, :]
-        else:
-            acc_out[h] = acc
-            tot_out[h] = tot
-            top_out[h] = top
-
-
-def attend_part(lengths, place, q, parts, state=None, final=False, lo=0, hi=ROWS):
+
+    def scores(h, m):
+        qq = jnp.concatenate([q_ref[:, h * DIM : (h + 1) * DIM], qa_ref[...]], axis=1)
+        return jnp.dot(qq, ka_ref[:, : m * ROWS], preferred_element_type=F32)
+
+    def fold(m):
+        ahead = scores(0, m) if m else None
+        for h in range(HEADS):
+            cols = slice(h * DIM, (h + 1) * DIM)
+            if m:
+                s = ahead
+                if h + 1 < HEADS:
+                    ahead = scores(h + 1, m)
+                parts = []
+                for b in range(m):
+                    c = s[:, b * ROWS : (b + 1) * ROWS]
+                    if kinds[b] == ("z", 0):
+                        r_id = own_row(lax.broadcasted_iota(jnp.int32, (ROWS, ROWS), 0), y, core)
+                        c_id = lax.broadcasted_iota(jnp.int32, (ROWS, ROWS), 1)
+                        c = jnp.where(c_id <= r_id, c, -BIG)
+                    parts += [c[:, :DIM], c[:, DIM:]]
+                top = parts[0]
+                for c in parts[1:]:
+                    top = jnp.maximum(top, c)
+                top = jnp.broadcast_to(jnp.max(top, axis=1, keepdims=True), (ROWS, DIM))
+                if not opening:
+                    old = state_in[2][h]
+                    top = jnp.maximum(old, top)
+                    keep = jnp.exp2((old - top) * SCALE)
+                p = [jnp.exp2((c - top) * SCALE).astype(BF16) for c in parts]
+                mixed = jnp.dot(
+                    jnp.concatenate(p, axis=1), va_ref[: m * ROWS, :], preferred_element_type=F32
+                )
+                acc, tot = mixed[:, :DIM], mixed[:, DIM:]
+                if not opening:
+                    acc = acc + state_in[0][h] * keep
+                    tot = tot + state_in[1][h] * keep
+            else:
+                acc, tot = state_in[0][h], state_in[1][h]
+            if final:
+                res = (acc / tot).astype(BF16)
+                for i, out in enumerate(outs):
+                    out[:, cols] = res[i * 2 * SHARE : (i + 1) * 2 * SHARE, :]
+            else:
+                acc_out[h] = acc
+                tot_out[h] = tot
+                top_out[h] = top
+
+    if final:
+        sizes = (0, 2, n)
+        for i, m in enumerate(sizes):
+            fits = front <= m
+            if i:
+                fits = fits & (front > sizes[i - 1])
+            pl.when(fits)(functools.partial(fold, m))
+    else:
+        fold(n)
+
+
+def attend_part(lengths, place, q, parts, state=None, final=False):
     kinds = tuple(k for ks, _ in parts for k in ks)
     n = len(kinds)
     opening = state is None
@@ -145,21 +185,21 @@
     arrays += list(state or ())
     part = jax.ShapeDtypeStruct((HEADS, ROWS, DIM), F32)
     if final:
-        outs = [jax.ShapeDtypeStruct((2 * SHARE, HEADS * DIM), BF16)] * ((hi - lo) // (2 * SHARE))
+        outs = [jax.ShapeDtypeStruct((2 * SHARE, HEADS * DIM), BF16)] * NY
     else:
         outs = [part] * 3
         if opening:
             outs += [jax.ShapeDtypeStruct((ROWS, HEADS * DIM), BF16), jax.ShapeDtypeStruct((ROWS, DIM), BF16)]
     return pl.pallas_call(
-        functools.partial(attend, kinds, lo, hi, opening, final),
+        functools.partial(attend, kinds, opening, final),
         out_shape=outs,
         in_specs=[SMEM, SMEM] + [VMEM] * len(arrays),
         out_specs=[VMEM] * len(outs),
-        scratch_shapes=[pltpu.VMEM((n * ROWS, 2 * DIM), BF16)] * 2,
+        scratch_shapes=[pltpu.VMEM((2 * DIM, n * ROWS), BF16), pltpu.VMEM((n * ROWS, 2 * DIM), BF16)],
         cost_estimate=pl.CostEstimate(
-            flops=8 * HEADS * (hi - lo) * ROWS * DIM * n,
+            flops=8 * HEADS * ROWS * ROWS * DIM * n,
             bytes_accessed=1 << 20,
-            transcendentals=HEADS * (hi - lo) * ROWS * n,
+            transcendentals=HEADS * ROWS * ROWS * n,
         ),
         compiler_params=pltpu.CompilerParams(vmem_limit_bytes=40 * 2**20),
         name="attend",
@@ -215,24 +255,24 @@
     one = send(own, perm=down)
     across = send(own, perm=flip(2))
     two = send(one, perm=down)
+    p_own = ((("z", 0),), own)
+    p_one = ((("z", 1),), one)
+    *state, qp, qa = attend_part(doc_lengths, where, (queries,), [p_own])
+    two, state = lax.optimization_barrier((two, state))
     one_across = send(across, perm=down)
     low = jnp.stack([one, jnp.where(x & 1 == 0, own, two)])
     high = jnp.stack([one, jnp.where(x & 2 == 0, own, two)])
     near = send(low, perm=flip(1))
     far = send(high, perm=flip(3))
     two_across = send(one_across, perm=down)
-    p_own = ((("z", 0),), own)
-    p_one = ((("z", 1),), one)
     p_two = ((("z", 2),), two)
     p_across = ((("row", 2),), one_across)
     p_near = ((("row", 1), ("mix", 1)), near)
     p_far = ((("row", 3), ("mix", 3)), far)
     p_either = ((("either", 2),), (across, two_across))
-    groups = [[p_own, p_one], [p_two, p_across], [p_near, p_far, p_either]]
-    *state, qp, qa = attend_part(doc_lengths, where, (queries,), groups[0])
-    for g in groups[1:-1]:
-        state = attend_part(doc_lengths, where, (qp, qa), g, state)
-    pieces = attend_part(doc_lengths, where, (qp, qa), groups[-1], state, True)
+    state = attend_part(doc_lengths, where, (qp, qa), [p_one, p_two, p_across], state)
+    last = [p_near, p_far, p_either]
+    pieces = attend_part(doc_lengths, where, (qp, qa), last, state, True)
     return exchange(where, pieces)
 
 

time: 46.9 us -> 42.4 us (0.904); the launches traced: 46.7 us -> 41.6 us
  Pallas kernels: 11.4 us -> 7.48 us
  local copies, waits for them, and re-layouts: 0.39 us -> 1.65 us
  starting transfers between devices: 18.3 us -> 17.1 us
  waiting for transfers between devices: 15.2 us -> 14.1 us
    pallas_call x3, Pallas kernels: 10 us -> 6.09 us  [attend_part(): pl.pallas_call(functools.partial(attend, kinds, opening, final), out_shap...]
    ppermute x1, waiting for transfers between devices: 5.01 us -> 1.61 us  [per_device(): two = send(one, perm=down)]
    ppermute x1, waiting for transfers between devices: 0.01 us -> 1.99 us  [per_device(): two_across = send(one_across, perm=down)]
    unnamed x8, local copies, waits for them, and re-layouts: 0.37 us -> 1.63 us
    ppermute x1, starting transfers between devices: 6.19 us -> 5.07 us  [exchange(): got = lax.ppermute(jnp.stack([h[SHARE:] for h in held]), 'kvh', flip(1))]
  transfers between devices with their start and end apart: 11 -> 11, of which waited for: 5 -> 7; matrix products, arithmetic and copies ran while one was open for 0% -> 0% of each run, Pallas kernels for 11% -> 12%
where the time goes in v3:
time: 42.4 us; the launch traced here: 41.6 us
  starting transfers between devices  17.1 us (40%)
  waiting for transfers between devices  14.1 us (33%)
  Pallas kernels  7.48 us (18%)
  local copies, waits for them, and re-layouts  1.65 us (4%)
  other arithmetic  1.06 us (2%)
    pallas_call x3, Pallas kernels, attend_part(): pl.pallas_call(functools.partial(attend, kinds, opening, final), out_shap...  6.09 us
    ppermute x1, starting transfers between devices, exchange(): got = lax.ppermute(jnp.stack([h[SHARE:] for h in held]), 'kvh', flip(1))  5.07 us
    ppermute x3, waiting for transfers between devices, exchange(): held[d] = lax.ppermute(pieces[d], 'kvh', flip(2 * d))  4.67 us
    ppermute x1, waiting for transfers between devices, per_device(): one = send(own, perm=down)  4.42 us
    ppermute x3, starting transfers between devices, exchange(): held[d] = lax.ppermute(pieces[d], 'kvh', flip(2 * d))  3.5 us
    ppermute x1, starting transfers between devices, per_device(): across = send(own, perm=flip(2))  2.74 us
    ppermute x1, starting transfers between devices, per_device(): one = send(own, perm=down)  2.54 us
    ppermute x1, waiting for transfers between devices, per_device(): two_across = send(one_across, perm=down)  1.99 us
  transfers between devices with their start and end apart: 11, of which 7 were waited for; matrix products, arithmetic and copies ran while one was open for 0% of the time, Pallas kernels for 12%

profile of v3, /device:TPU:1, one launch (start us, length us, event | category | flops | bytes accessed | tf_op | source)
XLA Modules:
  0.0 41.6 jit_solution(513758610170577125)
XLA Ops:
  0.0 0.9 %pad_maximum_fusion.3.refs_3_ = bf16[2,256,128]{2,1,0:T(8,128)(2,1)S(1)} fusion(bf16[1,256,128]{2,1,0:T(8,128)(2,1)} %bitcast.19, bf16[1,256,128]{2,1,0:T(8,128)(2,1)} %bitcast.21), kind=kLoop, calls=%fused_computation.3 | loop fusion | flops 65536 | bytes 262144 | tf_op jit(solution)/shard_map/stack | solution.py:254
  0.9 2.5 %collective-permute-start = (bf16[2,256,128]{2,1,0:T(8,128)(2,1)S(1)}, bf16[2,256,128]{2,1,0:T(8,128)(2,1)S(1)}, u32[]{:S(2)}, u32[]{:S(2)}) collective-permute-start(bf16[2,256,128]{2,1,0:T(8,128)(2,1)S(1)} %pad_maximum_fusion.3.refs_3_), channel_id=1, source_target_pairs={{0,32},{8,40},{16,48},{24,56},{32,64},{40,72},{48,80},{56,88},{64,... | collective-permute-start | bytes 393224 | tf_op jit(solution)/shard_map/ppermute | solution.py:255
  3.4 2.7 %collective-permute-start.4 = (bf16[2,256,128]{2,1,0:T(8,128)(2,1)S(1)}, bf16[2,256,128]{2,1,0:T(8,128)(2,1)S(1)}, u32[]{:S(2)}, u32[]{:S(2)}) collective-permute-start(bf16[2,256,128]{2,1,0:T(8,128)(2,1)S(1)} %pad_maximum_fusion.3.refs_3_), channel_id=1, source_target_pairs={{0,16},{8,24},{16,0},{24,8},{32,48},{40,56},{48,32},{56,40},{64,80... | collective-permute-start | bytes 393224 | tf_op jit(solution)/shard_map/ppermute | solution.py:256
  6.2 4.4 %collective-permute-done.refs_4_ = bf16[2,256,128]{2,1,0:T(8,128)(2,1)S(1)} collective-permute-done((bf16[2,256,128]{2,1,0:T(8,128)(2,1)S(1)}, bf16[2,256,128]{2,1,0:T(8,128)(2,1)S(1)}, u32[]{:S(2)}, u32[]{:S(2)}) %collective-permute-start) | collective-permute-done | bytes 131104 | tf_op jit(solution)/shard_map/ppermute | solution.py:255
  10.6 0.1 pad_add_fusion.refs_1_.place_ref
  10.7 0.6 %copy-done.1 = s32[16]{0:T(128)S(1)} copy-done((s32[16]{0:T(128)S(1)}, s32[16]{0:T(128)}, u32[]{:S(2)}) %copy-start.1) | copy-done | bytes 88
  11.3 1.0 %copy-done = bf16[256,1024]{1,0:T(8,128)(2,1)S(1)} copy-done((bf16[256,1024]{1,0:T(8,128)(2,1)S(1)}, bf16[256,1024]{1,0:T(8,128)(2,1)}, u32[]{:S(2)}) %copy-start) | copy-done | bytes 524312
  12.3 1.6 %attend.3 = (f32[8,256,128]{2,1,0:T(8,128)S(1)}, f32[8,256,128]{2,1,0:T(8,128)S(1)}, f32[8,256,128]{2,1,0:T(8,128)S(1)}, bf16[256,1024]{1,0:T(8,128)(2,1)S(1)}, bf16[256,128]{1,0:T(8,128)(2,1)S(1)}) custom-call(s32[16]{0:T(128)S(1)} %copy-done.1, s32[3]{0:T(128)S(1)} %pad_add_fusion.refs_1_.place_ref, bf16[256,1024]{1,0:T(8,128)(2,1)S(1)} %copy-done, ...), custom_call_target="tpu_custom_call" | custom-call | flops 536870912 | bytes 1048576 | tf_op jit(solution)/shard_map/attend/pallas_call | solution.py:193
  13.9 0.1 collective-permute-start.5
  14.0 1.6 %collective-permute-done.1.refs_5_ = bf16[2,256,128]{2,1,0:T(8,128)(2,1)S(1)} collective-permute-done((bf16[2,256,128]{2,1,0:T(8,128)(2,1)S(1)}, bf16[2,256,128]{2,1,0:T(8,128)(2,1)S(1)}, u32[]{:S(2)}, u32[]{:S(2)}) %collective-permute-start.1) | collective-permute-done | bytes 131104 | tf_op jit(solution)/shard_map/ppermute | solution.py:257
  15.7 1.3 %collective-permute-start.2 = (bf16[2,2,256,128]{3,2,1,0:T(8,128)(2,1)S(1)}, bf16[2,2,256,128]{3,2,1,0:T(8,128)(2,1)S(1)}, u32[]{:S(2)}, u32[]{:S(2)}) collective-permute-start(bf16[2,2,256,128]{3,2,1,0:T(8,128)(2,1)S(1)} %get-tuple-element.40), channel_id=1, source_target_pairs={{0,8},{8,0},{16,24},{24,16},{32,40},{40,32},{48,56},{56,48},{64,72... | collective-permute-start | bytes 786440 | tf_op jit(solution)/shard_map/ppermute | solution.py:265
  17.0 1.8 %collective-permute-start.3 = (bf16[2,2,256,128]{3,2,1,0:T(8,128)(2,1)S(1)}, bf16[2,2,256,128]{3,2,1,0:T(8,128)(2,1)S(1)}, u32[]{:S(2)}, u32[]{:S(2)}) collective-permute-start(bf16[2,2,256,128]{3,2,1,0:T(8,128)(2,1)S(1)} %get-tuple-element.39), channel_id=1, source_target_pairs={{0,24},{8,16},{16,8},{24,0},{32,56},{40,48},{48,40},{56,32},{64,88... | collective-permute-start | bytes 786440 | tf_op jit(solution)/shard_map/ppermute | solution.py:266
  18.8 0.2 collective-permute-done.5.refs_6_
  19.0 3.3 %attend.4 = (f32[8,256,128]{2,1,0:T(8,128)S(1)}, f32[8,256,128]{2,1,0:T(8,128)S(1)}, f32[8,256,128]{2,1,0:T(8,128)S(1)}) custom-call(s32[16]{0:T(128)S(1)} %copy-done.1, s32[3]{0:T(128)S(1)} %pad_add_fusion.refs_1_.place_ref, bf16[256,1024]{1,0:T(8,128)(2,1)S(1)} %get-tuple-element.21.refs_2_, bf16[256,128]{1,0:T(8,128)(2,1)S(1)} %get-tuple-element.22.refs_3_, ...), custom_call_target="tpu_custom_call" | custom-call | flops 1610612736 | bytes 1048576 | tf_op jit(solution)/shard_map/attend/pallas_call | solution.py:193
  22.4 2.0 %collective-permute-done.6.refs_7_ = bf16[2,256,128]{2,1,0:T(8,128)(2,1)S(1)} collective-permute-done((bf16[2,256,128]{2,1,0:T(8,128)(2,1)S(1)}, bf16[2,256,128]{2,1,0:T(8,128)(2,1)S(1)}, u32[]{:S(2)}, u32[]{:S(2)}) %collective-permute-start.6) | collective-permute-done | bytes 131104 | tf_op jit(solution)/shard_map/ppermute | solution.py:267
  24.4 1.2 %attend.5 = (bf16[64,1024]{1,0:T(8,128)(2,1)S(1)}, bf16[64,1024]{1,0:T(8,128)(2,1)S(1)}, bf16[64,1024]{1,0:T(8,128)(2,1)S(1)}, bf16[64,1024]{1,0:T(8,128)(2,1)S(1)}) custom-call(s32[16]{0:T(128)S(1)} %copy-done.1, s32[3]{0:T(128)S(1)} %pad_add_fusion.refs_1_.place_ref, bf16[256,1024]{1,0:T(8,128)(2,1)S(1)} %get-tuple-element.21.refs_2_, ...), custom_call_target="tpu_custom_call" | custom-call | flops 2684354560 | bytes 1048576 | tf_op jit(solution)/shard_map/attend/pallas_call | solution.py:193
  25.5 2.8 %collective-permute-start.9 = (bf16[64,1024]{1,0:T(8,128)(2,1)S(1)}, bf16[64,1024]{1,0:T(8,128)(2,1)S(1)}, u32[]{:S(2)}, u32[]{:S(2)}) collective-permute-start(bf16[64,1024]{1,0:T(8,128)(2,1)S(1)} %get-tuple-element.36), channel_id=1, source_target_pairs={{0,6},{1,7},{2,4},{3,5},{4,2},{5,3},{6,0},{7,1},{8,14},{9,15},{10,... | collective-permute-start | bytes 393224 | tf_op jit(solution)/shard_map/ppermute | solution.py:230
  28.4 0.3 collective-permute-start.8
  28.7 0.3 collective-permute-start.7
  29.0 2.6 %collective-permute-done.9.refs_3_ = bf16[64,1024]{1,0:T(8,128)(2,1)S(1)} collective-permute-done((bf16[64,1024]{1,0:T(8,128)(2,1)S(1)}, bf16[64,1024]{1,0:T(8,128)(2,1)S(1)}, u32[]{:S(2)}, u32[]{:S(2)}) %collective-permute-start.9) | collective-permute-done | bytes 131104 | tf_op jit(solution)/shard_map/ppermute | solution.py:230
  31.7 2.0 %collective-permute-done.8.refs_2_ = bf16[64,1024]{1,0:T(8,128)(2,1)S(1)} collective-permute-done((bf16[64,1024]{1,0:T(8,128)(2,1)S(1)}, bf16[64,1024]{1,0:T(8,128)(2,1)S(1)}, u32[]{:S(2)}, u32[]{:S(2)}) %collective-permute-start.8) | collective-permute-done | bytes 131104 | tf_op jit(solution)/shard_map/ppermute | solution.py:230
  33.8 5.1 %collective-permute-start.10 = (bf16[4,32,1024]{2,1,0:T(8,128)(2,1)S(1)}, bf16[4,32,1024]{2,1,0:T(8,128)(2,1)S(1)}, u32[]{:S(2)}, u32[]{:S(2)}) collective-permute-start(bf16[4,32,1024]{2,1,0:T(8,128)(2,1)S(1)} %pad_maximum_fusion.2), channel_id=1, source_target_pairs={{0,1},{1,0},{2,3},{3,2},{4,5},{5,4},{6,7},{7,6},{8,9},{9,8},{10,11... | collective-permute-start | bytes 786440 | tf_op jit(solution)/shard_map/ppermute | solution.py:232
  38.9 1.2 %collective-permute-done.10.refs_4_ = bf16[4,32,1024]{2,1,0:T(8,128)(2,1)S(1)} collective-permute-done((bf16[4,32,1024]{2,1,0:T(8,128)(2,1)S(1)}, bf16[4,32,1024]{2,1,0:T(8,128)(2,1)S(1)}, u32[]{:S(2)}, u32[]{:S(2)}) %collective-permute-start.10) | collective-permute-done | bytes 262176 | tf_op jit(solution)/shard_map/ppermute | solution.py:232
  40.0 1.4 %lay_out.1 = bf16[32,8192]{1,0:T(8,128)(2,1)} custom-call(s32[3]{0:T(128)S(1)} %pad_add_fusion.refs_1_.place_ref, bf16[64,1024]{1,0:T(8,128)(2,1)S(1)} %get-tuple-element.33.refs_0_, bf16[64,1024]{1,0:T(8,128)(2,1)S(1)} %collective-permute-done.7.refs_1_, bf16[64,1024]{1,0:T(8,128)(2,1)S(1)} %collective-permute-done.8.refs_2_, ...), custom_call_target="tpu_custom_call" | custom-call | tf_op jit(solution)/shard_map/lay_out/pallas_call | solution.py:234
  (19 shorter events, 0.2 us)
Async XLA Ops:
  0.9 9.7 %collective-permute-start = (bf16[2,256,128]{2,1,0:T(8,128)(2,1)S(1)}, bf16[2,256,128]{2,1,0:T(8,128)(2,1)S(1)}, u32[]{:S(2)}, u32[]{:S(2)}) collective-permute-start(bf16[2,256,128]{2,1,0:T(8,128)(2,1)S(1)} %pad_maximum_fusion.3.refs_3_), channel_id=1, source_target_pairs={{0,32},{8,40},{16,48},{24,56},{32,64},{40,72},{48,80},{56,88},{64,... | collective-permute-start | bytes 393224 | tf_op jit(solution)/shard_map/ppermute | solution.py:255
  3.4 10.5 %collective-permute-start.4 = (bf16[2,256,128]{2,1,0:T(8,128)(2,1)S(1)}, bf16[2,256,128]{2,1,0:T(8,128)(2,1)S(1)}, u32[]{:S(2)}, u32[]{:S(2)}) collective-permute-start(bf16[2,256,128]{2,1,0:T(8,128)(2,1)S(1)} %pad_maximum_fusion.3.refs_3_), channel_id=1, source_target_pairs={{0,16},{8,24},{16,0},{24,8},{32,48},{40,56},{48,32},{56,40},{64,80... | collective-permute-start | bytes 393224 | tf_op jit(solution)/shard_map/ppermute | solution.py:256
  10.6 5.0 %collective-permute-start.1 = (bf16[2,256,128]{2,1,0:T(8,128)(2,1)S(1)}, bf16[2,256,128]{2,1,0:T(8,128)(2,1)S(1)}, u32[]{:S(2)}, u32[]{:S(2)}) collective-permute-start(bf16[2,256,128]{2,1,0:T(8,128)(2,1)S(1)} %collective-permute-done.refs_4_), channel_id=1, source_target_pairs={{0,32},{8,40},{16,48},{24,56},{32,64},{40,72},{48,80},{56,88},{64,... | collective-permute-start | bytes 393224 | tf_op jit(solution)/shard_map/ppermute | solution.py:257
  10.6 0.7 %copy-start.1 = (s32[16]{0:T(128)S(1)}, s32[16]{0:T(128)}, u32[]{:S(2)}) copy-start(s32[16]{0:T(128)} %refs_0_.5) | copy-start | bytes 196
  11.3 1.0 %copy-start = (bf16[256,1024]{1,0:T(8,128)(2,1)S(1)}, bf16[256,1024]{1,0:T(8,128)(2,1)}, u32[]{:S(2)}) copy-start(bf16[256,1024]{1,0:T(8,128)(2,1)} %refs_2_.1) | copy-start | bytes 1572868
  12.3 3.3 %copy-start.2 = (bf16[256,128]{1,0:T(8,128)(2,1)S(1)}, bf16[256,128]{1,0:T(8,128)(2,1)}, u32[]{:S(2)}) copy-start(bf16[256,128]{1,0:T(8,128)(2,1)} %param.6) | copy-start | bytes 196612
  12.3 3.3 %copy-start.3 = (bf16[256,128]{1,0:T(8,128)(2,1)S(1)}, bf16[256,128]{1,0:T(8,128)(2,1)}, u32[]{:S(2)}) copy-start(bf16[256,128]{1,0:T(8,128)(2,1)} %param.5) | copy-start | bytes 196612
  13.9 5.1 %collective-permute-start.5 = (bf16[2,256,128]{2,1,0:T(8,128)(2,1)S(1)}, bf16[2,256,128]{2,1,0:T(8,128)(2,1)S(1)}, u32[]{:S(2)}, u32[]{:S(2)}) collective-permute-start(bf16[2,256,128]{2,1,0:T(8,128)(2,1)S(1)} %collective-permute-done.4.refs_6_), channel_id=1, source_target_pairs={{0,32},{8,40},{16,48},{24,56},{32,64},{40,72},{48,80},{56,88},{64,... | collective-permute-start | bytes 393224 | tf_op jit(solution)/shard_map/ppermute | solution.py:262
  15.7 8.6 %collective-permute-start.2 = (bf16[2,2,256,128]{3,2,1,0:T(8,128)(2,1)S(1)}, bf16[2,2,256,128]{3,2,1,0:T(8,128)(2,1)S(1)}, u32[]{:S(2)}, u32[]{:S(2)}) collective-permute-start(bf16[2,2,256,128]{3,2,1,0:T(8,128)(2,1)S(1)} %get-tuple-element.40), channel_id=1, source_target_pairs={{0,8},{8,0},{16,24},{24,16},{32,40},{40,32},{48,56},{56,48},{64,72... | collective-permute-start | bytes 786440 | tf_op jit(solution)/shard_map/ppermute | solution.py:265
  17.0 7.4 %collective-permute-start.3 = (bf16[2,2,256,128]{3,2,1,0:T(8,128)(2,1)S(1)}, bf16[2,2,256,128]{3,2,1,0:T(8,128)(2,1)S(1)}, u32[]{:S(2)}, u32[]{:S(2)}) collective-permute-start(bf16[2,2,256,128]{3,2,1,0:T(8,128)(2,1)S(1)} %get-tuple-element.39), channel_id=1, source_target_pairs={{0,24},{8,16},{16,8},{24,0},{32,56},{40,48},{48,40},{56,32},{64,88... | collective-permute-start | bytes 786440 | tf_op jit(solution)/shard_map/ppermute | solution.py:266
  19.0 5.3 %collective-permute-start.6 = (bf16[2,256,128]{2,1,0:T(8,128)(2,1)S(1)}, bf16[2,256,128]{2,1,0:T(8,128)(2,1)S(1)}, u32[]{:S(2)}, u32[]{:S(2)}) collective-permute-start(bf16[2,256,128]{2,1,0:T(8,128)(2,1)S(1)} %collective-permute-done.5.refs_6_), channel_id=1, source_target_pairs={{0,32},{8,40},{16,48},{24,56},{32,64},{40,72},{48,80},{56,88},{64,... | collective-permute-start | bytes 393224 | tf_op jit(solution)/shard_map/ppermute | solution.py:267
  25.5 6.1 %collective-permute-start.9 = (bf16[64,1024]{1,0:T(8,128)(2,1)S(1)}, bf16[64,1024]{1,0:T(8,128)(2,1)S(1)}, u32[]{:S(2)}, u32[]{:S(2)}) collective-permute-start(bf16[64,1024]{1,0:T(8,128)(2,1)S(1)} %get-tuple-element.36), channel_id=1, source_target_pairs={{0,6},{1,7},{2,4},{3,5},{4,2},{5,3},{6,0},{7,1},{8,14},{9,15},{10,... | collective-permute-start | bytes 393224 | tf_op jit(solution)/shard_map/ppermute | solution.py:230
  28.4 5.4 %collective-permute-start.8 = (bf16[64,1024]{1,0:T(8,128)(2,1)S(1)}, bf16[64,1024]{1,0:T(8,128)(2,1)S(1)}, u32[]{:S(2)}, u32[]{:S(2)}) collective-permute-start(bf16[64,1024]{1,0:T(8,128)(2,1)S(1)} %get-tuple-element.35), channel_id=1, source_target_pairs={{0,4},{1,5},{2,6},{3,7},{4,0},{5,1},{6,2},{7,3},{8,12},{9,13},{10,... | collective-permute-start | bytes 393224 | tf_op jit(solution)/shard_map/ppermute | solution.py:230
  28.7 5.0 %collective-permute-start.7 = (bf16[64,1024]{1,0:T(8,128)(2,1)S(1)}, bf16[64,1024]{1,0:T(8,128)(2,1)S(1)}, u32[]{:S(2)}, u32[]{:S(2)}) collective-permute-start(bf16[64,1024]{1,0:T(8,128)(2,1)S(1)} %get-tuple-element.34), channel_id=1, source_target_pairs={{0,2},{1,3},{2,0},{3,1},{4,6},{5,7},{6,4},{7,5},{8,10},{9,11},{10,... | collective-permute-start | bytes 393224 | tf_op jit(solution)/shard_map/ppermute | solution.py:230
  33.8 6.2 %collective-permute-start.10 = (bf16[4,32,1024]{2,1,0:T(8,128)(2,1)S(1)}, bf16[4,32,1024]{2,1,0:T(8,128)(2,1)S(1)}, u32[]{:S(2)}, u32[]{:S(2)}) collective-permute-start(bf16[4,32,1024]{2,1,0:T(8,128)(2,1)S(1)} %pad_maximum_fusion.2), channel_id=1, source_target_pairs={{0,1},{1,0},{2,3},{3,2},{4,5},{5,4},{6,7},{7,6},{8,9},{9,8},{10,11... | collective-permute-start | bytes 786440 | tf_op jit(solution)/shard_map/ppermute | solution.py:232

commit v4 on v3

--- a/solution.py
+++ b/solution.py
@@ -37,6 +37,11 @@
     return first, last
 
 
+def position():
+    kvh = lax.axis_index("kvh").astype(jnp.int32)
+    return lax.axis_index("ctx").astype(jnp.int32), kvh // 2, kvh % 2
+
+
 def reach(len_ref, place):
     at = jnp.int32(0)
     begin = jnp.int32(0)
@@ -62,9 +67,9 @@
 
 def attend(kinds, opening, final, *refs):
     n = len(kinds)
-    len_ref, place_ref = refs[:2]
-    rest = list(refs[2:])
-    place, y, core = place_ref[0], place_ref[1], place_ref[2]
+    len_ref = refs[0]
+    rest = list(refs[1:])
+    place, y, core = position()
     x = lax.rem(place, NX)
     q_ref = rest.pop(0)
     if not opening:
@@ -95,27 +100,31 @@
         pos = place * ROWS + own_row(lax.broadcasted_iota(jnp.int32, (ROWS, DIM), 0), y, core)
         qa_ref[...] = jnp.where((pos >= first) & (pos < last), 0.0, -BIG).astype(BF16)
         q_ref = qp_ref
-    front, back = jnp.int32(0), jnp.int32(n - 1)
+    front = jnp.int32(0)
     begin = reach(len_ref, place)
+    va_ref[:, DIM:] = jnp.ones((n * ROWS, DIM), BF16)
     for b, (kind, d) in enumerate(kinds):
-        if kind == "either":
-            late = x < (x ^ d)
-            key = jnp.where(late, kv[b][1][0], kv[b][0][0])
-            val = jnp.where(late, kv[b][1][1], kv[b][0][1])
+        start = block_of(kind, d, place, x) * ROWS
+
+        def place_block(at, b=b, kind=kind, d=d, start=start):
+            if kind == "either":
+                late = x < (x ^ d)
+                key = jnp.where(late, kv[b][1][0], kv[b][0][0])
+                val = jnp.where(late, kv[b][1][1], kv[b][0][1])
+            else:
+                key, val = kv[b][0], kv[b][1]
+            pos = start + lax.broadcasted_iota(jnp.int32, (ROWS, DIM), 0)
+            ka_ref[:DIM, at] = key.T
+            ka_ref[DIM:, at] = jnp.where((pos >= first) & (pos < last), 1.0, 0.0).astype(BF16).T
+            va_ref[at, :DIM] = val
+
+        if opening:
+            place_block(slice(b * ROWS, (b + 1) * ROWS))
         else:
-            key, val = kv[b][0], kv[b][1]
-        start = block_of(kind, d, place, x) * ROWS
-        rows = slice(b * ROWS, (b + 1) * ROWS)
-        at = rows
-        if final:
-            used = (start + ROWS > begin).astype(jnp.int32)
-            at = pl.ds(pl.multiple_of(jnp.where(used == 1, front, back) * ROWS, ROWS), ROWS)
-            front, back = front + used, back - (1 - used)
-        pos = start + lax.broadcasted_iota(jnp.int32, (ROWS, DIM), 0)
-        ka_ref[:DIM, at] = key.T
-        ka_ref[DIM:, at] = jnp.where((pos >= first) & (pos < last), 1.0, 0.0).astype(BF16).T
-        va_ref[at, :DIM] = val
-        va_ref[rows, DIM:] = jnp.ones((ROWS, DIM), BF16)
+            used = start + ROWS > begin
+            at = pl.ds(pl.multiple_of(front * ROWS, ROWS), ROWS)
+            pl.when(used)(functools.partial(place_block, at))
+            front = front + used.astype(jnp.int32)
 
     def scores(h, m):
         qq = jnp.concatenate([q_ref[:, h * DIM : (h + 1) * DIM], qa_ref[...]], axis=1)
@@ -154,7 +163,7 @@
                     acc = acc + state_in[0][h] * keep
                     tot = tot + state_in[1][h] * keep
             else:
-                acc, tot = state_in[0][h], state_in[1][h]
+                acc, tot, top = state_in[0][h], state_in[1][h], state_in[2][h]
             if final:
                 res = (acc / tot).astype(BF16)
                 for i, out in enumerate(outs):
@@ -164,18 +173,14 @@
                 tot_out[h] = tot
                 top_out[h] = top
 
-    if final:
-        sizes = (0, 2, n)
-        for i, m in enumerate(sizes):
-            fits = front <= m
-            if i:
-                fits = fits & (front > sizes[i - 1])
-            pl.when(fits)(functools.partial(fold, m))
+    if opening:
+        fold(n)
     else:
-        fold(n)
-
-
-def attend_part(lengths, place, q, parts, state=None, final=False):
+        for m in range(n + 1):
+            pl.when(front == m)(functools.partial(fold, m))
+
+
+def attend_part(lengths, q, parts, state=None, final=False):
     kinds = tuple(k for ks, _ in parts for k in ks)
     n = len(kinds)
     opening = state is None
@@ -193,7 +198,7 @@
     return pl.pallas_call(
         functools.partial(attend, kinds, opening, final),
         out_shape=outs,
-        in_specs=[SMEM, SMEM] + [VMEM] * len(arrays),
+        in_specs=[SMEM] + [VMEM] * len(arrays),
         out_specs=[VMEM] * len(outs),
         scratch_shapes=[pltpu.VMEM((2 * DIM, n * ROWS), BF16), pltpu.VMEM((n * ROWS, 2 * DIM), BF16)],
         cost_estimate=pl.CostEstimate(
@@ -201,13 +206,13 @@
             bytes_accessed=1 << 20,
             transcendentals=HEADS * ROWS * ROWS * n,
         ),
-        compiler_params=pltpu.CompilerParams(vmem_limit_bytes=40 * 2**20),
+        compiler_params=pltpu.CompilerParams(vmem_limit_bytes=16 * 2**20),
         name="attend",
-    )(lengths, place, *arrays)
-
-
-def lay_out(place_ref, *refs):
-    y, core = place_ref[1], place_ref[2]
+    )(lengths, *arrays)
+
+
+def lay_out(*refs):
+    _, y, core = position()
     pieces, got, out, sems = refs[:NY], refs[NY], refs[NY + 1], refs[NY + 2]
     width = HEADS * DIM
     copies = []
@@ -222,7 +227,7 @@
         c.wait()
 
 
-def exchange(place, pieces):
+def exchange(pieces):
     size = lax.axis_size("kvh")
     flip = lambda m: [(i, i ^ m) for i in range(size)]
     held = {0: pieces[0]}
@@ -234,12 +239,12 @@
     return pl.pallas_call(
         lay_out,
         out_shape=jax.ShapeDtypeStruct((SHARE, size * HEADS * DIM), BF16),
-        in_specs=[SMEM] + [VMEM] * (NY + 1),
+        in_specs=[VMEM] * (NY + 1),
         out_specs=anywhere,
         scratch_shapes=[pltpu.SemaphoreType.DMA((2 * NY,))],
-        compiler_params=pltpu.CompilerParams(vmem_limit_bytes=40 * 2**20),
+        compiler_params=pltpu.CompilerParams(vmem_limit_bytes=16 * 2**20),
         name="lay_out",
-    )(place, *held, got)
+    )(*held, got)
 
 
 def per_device(queries, keys, values, doc_lengths):
@@ -247,17 +252,16 @@
     down = [(i, (i + NX) % size) for i in range(size)]
     flip = lambda d: [(i, i ^ d) for i in range(size)]
     place = lax.axis_index("ctx")
-    kvh = lax.axis_index("kvh")
     x = place % NX
-    where = jnp.stack([place, kvh // 2, kvh % 2]).astype(jnp.int32)
     send = functools.partial(lax.ppermute, axis_name="ctx")
     own = jnp.stack([keys, values])
     one = send(own, perm=down)
     across = send(own, perm=flip(2))
     two = send(one, perm=down)
-    p_own = ((("z", 0),), own)
     p_one = ((("z", 1),), one)
-    *state, qp, qa = attend_part(doc_lengths, where, (queries,), [p_own])
+    across, mine = lax.optimization_barrier((across, own))
+    p_own = ((("z", 0),), mine)
+    *state, qp, qa = attend_part(doc_lengths, (queries,), [p_own])
     two, state = lax.optimization_barrier((two, state))
     one_across = send(across, perm=down)
     low = jnp.stack([one, jnp.where(x & 1 == 0, own, two)])
@@ -270,10 +274,10 @@
     p_near = ((("row", 1), ("mix", 1)), near)
     p_far = ((("row", 3), ("mix", 3)), far)
     p_either = ((("either", 2),), (across, two_across))
-    state = attend_part(doc_lengths, where, (qp, qa), [p_one, p_two, p_across], state)
+    state = attend_part(doc_lengths, (qp, qa), [p_one, p_two, p_across], state)
     last = [p_near, p_far, p_either]
-    pieces = attend_part(doc_lengths, where, (qp, qa), last, state, True)
-    return exchange(where, pieces)
+    pieces = attend_part(doc_lengths, (qp, qa), last, state, True)
+    return exchange(pieces)
 
 
 def solution(mesh):

time: 42.4 us -> 42.1 us (level); the launches traced: 41.6 us -> 41.9 us
  Pallas kernels: 7.48 us -> 4.21 us
  waiting for transfers between devices: 14.1 us -> 16.2 us
  starting transfers between devices: 17.1 us -> 18.7 us
    pallas_call x3, Pallas kernels: 6.09 us -> 3.37 us  [attend_part(): pl.pallas_call(functools.partial(attend, kinds, opening, final), out_shap...]
    ppermute x1, waiting for transfers between devices: 1.99 us -> 4.21 us  [per_device(): two_across = send(one_across, perm=down)]
    ppermute x1, starting transfers between devices: 5.07 us -> 6.72 us  [exchange(): got = lax.ppermute(jnp.stack([h[SHARE:] for h in held]), 'kvh', flip(1))]
    pallas_call x1, Pallas kernels: 1.39 us -> 0.85 us  [exchange(): pl.pallas_call(lay_out, out_shape=jax.ShapeDtypeStruct((SHARE, size * HEA...]
  transfers between devices with their start and end apart: 11 -> 11, of which waited for: 7 -> 6; matrix products, arithmetic and copies ran while one was open for 0% -> 0% of each run, Pallas kernels for 12% -> 6%
where the time goes in v4:
time: 42.1 us; the launch traced here: 41.9 us
  starting transfers between devices  18.7 us (44%)
  waiting for transfers between devices  16.2 us (38%)
  Pallas kernels  4.21 us (10%)
  local copies, waits for them, and re-layouts  1.63 us (4%)
  other arithmetic  0.99 us (2%)
    ppermute x1, starting transfers between devices, exchange(): got = lax.ppermute(jnp.stack([h[SHARE:] for h in held]), 'kvh', flip(1))  6.72 us
    ppermute x3, waiting for transfers between devices, exchange(): held[d] = lax.ppermute(pieces[d], 'kvh', flip(2 * d))  4.63 us
    ppermute x1, waiting for transfers between devices, per_device(): one = send(own, perm=down)  4.42 us
    ppermute x1, waiting for transfers between devices, per_device(): two_across = send(one_across, perm=down)  4.21 us
    ppermute x3, starting transfers between devices, exchange(): held[d] = lax.ppermute(pieces[d], 'kvh', flip(2 * d))  3.5 us
    pallas_call x3, Pallas kernels, attend_part(): pl.pallas_call(functools.partial(attend, kinds, opening, final), out_shap...  3.37 us
    ppermute x1, starting transfers between devices, per_device(): across = send(own, perm=flip(2))  2.74 us
    ppermute x1, starting transfers between devices, per_device(): one = send(own, perm=down)  2.54 us
  transfers between devices with their start and end apart: 11, of which 6 were waited for; matrix products, arithmetic and copies ran while one was open for 0% of the time, Pallas kernels for 6%

profile of v4, /device:TPU:1, one launch (start us, length us, event | category | flops | bytes accessed | tf_op | source)
XLA Modules:
  0.0 41.9 jit_solution(4288136022400677323)
XLA Ops:
  0.0 0.9 %pad_maximum_fusion.3.refs_2_ = bf16[2,256,128]{2,1,0:T(8,128)(2,1)S(1)} fusion(bf16[1,256,128]{2,1,0:T(8,128)(2,1)} %bitcast.16, bf16[1,256,128]{2,1,0:T(8,128)(2,1)} %bitcast.18), kind=kLoop, calls=%fused_computation.3 | loop fusion | flops 65536 | bytes 262144 | tf_op jit(solution)/shard_map/stack | solution.py:257
  0.9 2.5 %collective-permute-start.1 = (bf16[2,256,128]{2,1,0:T(8,128)(2,1)S(1)}, bf16[2,256,128]{2,1,0:T(8,128)(2,1)S(1)}, u32[]{:S(2)}, u32[]{:S(2)}) collective-permute-start(bf16[2,256,128]{2,1,0:T(8,128)(2,1)S(1)} %pad_maximum_fusion.3.refs_2_), channel_id=1, source_target_pairs={{0,32},{8,40},{16,48},{24,56},{32,64},{40,72},{48,80},{56,88},{64,... | collective-permute-start | bytes 393224 | tf_op jit(solution)/shard_map/ppermute | solution.py:258
  3.4 2.7 %collective-permute-start = (bf16[2,256,128]{2,1,0:T(8,128)(2,1)S(1)}, bf16[2,256,128]{2,1,0:T(8,128)(2,1)S(1)}, u32[]{:S(2)}, u32[]{:S(2)}) collective-permute-start(bf16[2,256,128]{2,1,0:T(8,128)(2,1)S(1)} %pad_maximum_fusion.3.refs_2_), channel_id=1, source_target_pairs={{0,16},{8,24},{16,0},{24,8},{32,48},{40,56},{48,32},{56,40},{64,80... | collective-permute-start | bytes 393224 | tf_op jit(solution)/shard_map/ppermute | solution.py:259
  6.2 4.4 %collective-permute-done.1.refs_3_ = bf16[2,256,128]{2,1,0:T(8,128)(2,1)S(1)} collective-permute-done((bf16[2,256,128]{2,1,0:T(8,128)(2,1)S(1)}, bf16[2,256,128]{2,1,0:T(8,128)(2,1)S(1)}, u32[]{:S(2)}, u32[]{:S(2)}) %collective-permute-start.1) | collective-permute-done | bytes 131104 | tf_op jit(solution)/shard_map/ppermute | solution.py:258
  10.6 0.0 collective-permute-start.2
  10.6 0.1 collective-permute-start.5
  10.7 0.6 %copy-done.1 = s32[16]{0:T(128)S(1)} copy-done((s32[16]{0:T(128)S(1)}, s32[16]{0:T(128)}, u32[]{:S(2)}) %copy-start.1) | copy-done | bytes 88
  11.3 1.0 %copy-done = bf16[256,1024]{1,0:T(8,128)(2,1)S(1)} copy-done((bf16[256,1024]{1,0:T(8,128)(2,1)S(1)}, bf16[256,1024]{1,0:T(8,128)(2,1)}, u32[]{:S(2)}) %copy-start) | copy-done | bytes 524312
  12.3 1.6 %attend.3 = (f32[8,256,128]{2,1,0:T(8,128)S(1)}, f32[8,256,128]{2,1,0:T(8,128)S(1)}, f32[8,256,128]{2,1,0:T(8,128)S(1)}, bf16[256,1024]{1,0:T(8,128)(2,1)S(1)}, bf16[256,128]{1,0:T(8,128)(2,1)S(1)}) custom-call(s32[16]{0:T(128)S(1)} %copy-done.1, bf16[256,1024]{1,0:T(8,128)(2,1)S(1)} %copy-done, bf16[2,256,128]{2,1,0:T(8,128)(2,1)S(1)} %pad_maximum_fusion.3.refs_2_), custom_call_target="tpu_custom_call" | custom-call | flops 536870912 | bytes 1048576 | tf_op jit(solution)/shard_map/attend/pallas_call | solution.py:198
  13.9 1.7 %collective-permute-done.2.refs_4_ = bf16[2,256,128]{2,1,0:T(8,128)(2,1)S(1)} collective-permute-done((bf16[2,256,128]{2,1,0:T(8,128)(2,1)S(1)}, bf16[2,256,128]{2,1,0:T(8,128)(2,1)S(1)}, u32[]{:S(2)}, u32[]{:S(2)}) %collective-permute-start.2) | collective-permute-done | bytes 131104 | tf_op jit(solution)/shard_map/ppermute | solution.py:260
  15.7 1.3 %collective-permute-start.3 = (bf16[2,2,256,128]{3,2,1,0:T(8,128)(2,1)S(1)}, bf16[2,2,256,128]{3,2,1,0:T(8,128)(2,1)S(1)}, u32[]{:S(2)}, u32[]{:S(2)}) collective-permute-start(bf16[2,2,256,128]{3,2,1,0:T(8,128)(2,1)S(1)} %get-tuple-element.44), channel_id=1, source_target_pairs={{0,8},{8,0},{16,24},{24,16},{32,40},{40,32},{48,56},{56,48},{64,72... | collective-permute-start | bytes 786440 | tf_op jit(solution)/shard_map/ppermute | solution.py:269
  17.0 1.8 %collective-permute-start.4 = (bf16[2,2,256,128]{3,2,1,0:T(8,128)(2,1)S(1)}, bf16[2,2,256,128]{3,2,1,0:T(8,128)(2,1)S(1)}, u32[]{:S(2)}, u32[]{:S(2)}) collective-permute-start(bf16[2,2,256,128]{3,2,1,0:T(8,128)(2,1)S(1)} %get-tuple-element.43), channel_id=1, source_target_pairs={{0,24},{8,16},{16,8},{24,0},{32,56},{40,48},{48,40},{56,32},{64,88... | collective-permute-start | bytes 786440 | tf_op jit(solution)/shard_map/ppermute | solution.py:270
  18.8 0.0 collective-permute-start.6
  18.8 0.8 %attend.4 = (f32[8,256,128]{2,1,0:T(8,128)S(1)}, f32[8,256,128]{2,1,0:T(8,128)S(1)}, f32[8,256,128]{2,1,0:T(8,128)S(1)}) custom-call(s32[16]{0:T(128)S(1)} %copy-done.1, bf16[256,1024]{1,0:T(8,128)(2,1)S(1)} %get-tuple-element.24.refs_1_, bf16[256,128]{1,0:T(8,128)(2,1)S(1)} %get-tuple-element.25.refs_2_, ...), custom_call_target="tpu_custom_call" | custom-call | flops 1610612736 | bytes 1048576 | tf_op jit(solution)/shard_map/attend/pallas_call | solution.py:198
  19.6 4.2 %collective-permute-done.6.refs_6_ = bf16[2,256,128]{2,1,0:T(8,128)(2,1)S(1)} collective-permute-done((bf16[2,256,128]{2,1,0:T(8,128)(2,1)S(1)}, bf16[2,256,128]{2,1,0:T(8,128)(2,1)S(1)}, u32[]{:S(2)}, u32[]{:S(2)}) %collective-permute-start.6) | collective-permute-done | bytes 131104 | tf_op jit(solution)/shard_map/ppermute | solution.py:271
  23.9 1.0 %attend.5 = (bf16[64,1024]{1,0:T(8,128)(2,1)S(1)}, bf16[64,1024]{1,0:T(8,128)(2,1)S(1)}, bf16[64,1024]{1,0:T(8,128)(2,1)S(1)}, bf16[64,1024]{1,0:T(8,128)(2,1)S(1)}) custom-call(s32[16]{0:T(128)S(1)} %copy-done.1, bf16[256,1024]{1,0:T(8,128)(2,1)S(1)} %get-tuple-element.24.refs_1_, bf16[256,128]{1,0:T(8,128)(2,1)S(1)} %get-tuple-element.25.refs_2_, ...), custom_call_target="tpu_custom_call" | custom-call | flops 2684354560 | bytes 1048576 | tf_op jit(solution)/shard_map/attend/pallas_call | solution.py:198
  24.8 2.8 %collective-permute-start.9 = (bf16[64,1024]{1,0:T(8,128)(2,1)S(1)}, bf16[64,1024]{1,0:T(8,128)(2,1)S(1)}, u32[]{:S(2)}, u32[]{:S(2)}) collective-permute-start(bf16[64,1024]{1,0:T(8,128)(2,1)S(1)} %get-tuple-element.40), channel_id=1, source_target_pairs={{0,6},{1,7},{2,4},{3,5},{4,2},{5,3},{6,0},{7,1},{8,14},{9,15},{10,... | collective-permute-start | bytes 393224 | tf_op jit(solution)/shard_map/ppermute | solution.py:235
  27.7 0.3 collective-permute-start.8
  28.0 0.3 collective-permute-start.7
  28.3 2.6 %collective-permute-done.9.refs_3_ = bf16[64,1024]{1,0:T(8,128)(2,1)S(1)} collective-permute-done((bf16[64,1024]{1,0:T(8,128)(2,1)S(1)}, bf16[64,1024]{1,0:T(8,128)(2,1)S(1)}, u32[]{:S(2)}, u32[]{:S(2)}) %collective-permute-start.9) | collective-permute-done | bytes 131104 | tf_op jit(solution)/shard_map/ppermute | solution.py:235
  31.0 2.0 %collective-permute-done.8.refs_2_ = bf16[64,1024]{1,0:T(8,128)(2,1)S(1)} collective-permute-done((bf16[64,1024]{1,0:T(8,128)(2,1)S(1)}, bf16[64,1024]{1,0:T(8,128)(2,1)S(1)}, u32[]{:S(2)}, u32[]{:S(2)}) %collective-permute-start.8) | collective-permute-done | bytes 131104 | tf_op jit(solution)/shard_map/ppermute | solution.py:235
  33.1 6.7 %collective-permute-start.10 = (bf16[4,32,1024]{2,1,0:T(8,128)(2,1)S(1)}, bf16[4,32,1024]{2,1,0:T(8,128)(2,1)S(1)}, u32[]{:S(2)}, u32[]{:S(2)}) collective-permute-start(bf16[4,32,1024]{2,1,0:T(8,128)(2,1)S(1)} %pad_maximum_fusion.2), channel_id=1, source_target_pairs={{0,1},{1,0},{2,3},{3,2},{4,5},{5,4},{6,7},{7,6},{8,9},{9,8},{10,11... | collective-permute-start | bytes 786440 | tf_op jit(solution)/shard_map/ppermute | solution.py:237
  39.8 1.2 %collective-permute-done.10.refs_4_ = bf16[4,32,1024]{2,1,0:T(8,128)(2,1)S(1)} collective-permute-done((bf16[4,32,1024]{2,1,0:T(8,128)(2,1)S(1)}, bf16[4,32,1024]{2,1,0:T(8,128)(2,1)S(1)}, u32[]{:S(2)}, u32[]{:S(2)}) %collective-permute-start.10) | collective-permute-done | bytes 262176 | tf_op jit(solution)/shard_map/ppermute | solution.py:237
  40.9 0.8 %lay_out.1 = bf16[32,8192]{1,0:T(8,128)(2,1)} custom-call(bf16[64,1024]{1,0:T(8,128)(2,1)S(1)} %get-tuple-element.37.refs_0_, bf16[64,1024]{1,0:T(8,128)(2,1)S(1)} %collective-permute-done.7.refs_1_, bf16[64,1024]{1,0:T(8,128)(2,1)S(1)} %collective-permute-done.8.refs_2_, bf16[64,1024]{1,0:T(8,128)(2,1)S(1)} %collective-permute-done.9.refs_3_, ...), custom_call_target="tpu_custom_call" | custom-call | tf_op jit(solution)/shard_map/lay_out/pallas_call | solution.py:239
  (18 shorter events, 0.1 us)
Async XLA Ops:
  0.9 9.7 %collective-permute-start.1 = (bf16[2,256,128]{2,1,0:T(8,128)(2,1)S(1)}, bf16[2,256,128]{2,1,0:T(8,128)(2,1)S(1)}, u32[]{:S(2)}, u32[]{:S(2)}) collective-permute-start(bf16[2,256,128]{2,1,0:T(8,128)(2,1)S(1)} %pad_maximum_fusion.3.refs_2_), channel_id=1, source_target_pairs={{0,32},{8,40},{16,48},{24,56},{32,64},{40,72},{48,80},{56,88},{64,... | collective-permute-start | bytes 393224 | tf_op jit(solution)/shard_map/ppermute | solution.py:258
  3.4 7.2 %collective-permute-start = (bf16[2,256,128]{2,1,0:T(8,128)(2,1)S(1)}, bf16[2,256,128]{2,1,0:T(8,128)(2,1)S(1)}, u32[]{:S(2)}, u32[]{:S(2)}) collective-permute-start(bf16[2,256,128]{2,1,0:T(8,128)(2,1)S(1)} %pad_maximum_fusion.3.refs_2_), channel_id=1, source_target_pairs={{0,16},{8,24},{16,0},{24,8},{32,48},{40,56},{48,32},{56,40},{64,80... | collective-permute-start | bytes 393224 | tf_op jit(solution)/shard_map/ppermute | solution.py:259
  10.6 5.0 %collective-permute-start.2 = (bf16[2,256,128]{2,1,0:T(8,128)(2,1)S(1)}, bf16[2,256,128]{2,1,0:T(8,128)(2,1)S(1)}, u32[]{:S(2)}, u32[]{:S(2)}) collective-permute-start(bf16[2,256,128]{2,1,0:T(8,128)(2,1)S(1)} %collective-permute-done.1.refs_3_), channel_id=1, source_target_pairs={{0,32},{8,40},{16,48},{24,56},{32,64},{40,72},{48,80},{56,88},{64,... | collective-permute-start | bytes 393224 | tf_op jit(solution)/shard_map/ppermute | solution.py:260
  10.6 0.7 %copy-start.1 = (s32[16]{0:T(128)S(1)}, s32[16]{0:T(128)}, u32[]{:S(2)}) copy-start(s32[16]{0:T(128)} %refs_0_.5) | copy-start | bytes 196
  10.6 8.2 %collective-permute-start.5 = (bf16[2,256,128]{2,1,0:T(8,128)(2,1)S(1)}, bf16[2,256,128]{2,1,0:T(8,128)(2,1)S(1)}, u32[]{:S(2)}, u32[]{:S(2)}) collective-permute-start(bf16[2,256,128]{2,1,0:T(8,128)(2,1)S(1)} %collective-permute-done.refs_5_), channel_id=1, source_target_pairs={{0,32},{8,40},{16,48},{24,56},{32,64},{40,72},{48,80},{56,88},{64,... | collective-permute-start | bytes 393224 | tf_op jit(solution)/shard_map/ppermute | solution.py:266
  11.3 1.0 %copy-start = (bf16[256,1024]{1,0:T(8,128)(2,1)S(1)}, bf16[256,1024]{1,0:T(8,128)(2,1)}, u32[]{:S(2)}) copy-start(bf16[256,1024]{1,0:T(8,128)(2,1)} %refs_1_.1) | copy-start | bytes 1572868
  12.3 3.3 %copy-start.2 = (bf16[256,128]{1,0:T(8,128)(2,1)S(1)}, bf16[256,128]{1,0:T(8,128)(2,1)}, u32[]{:S(2)}) copy-start(bf16[256,128]{1,0:T(8,128)(2,1)} %param.6) | copy-start | bytes 196612
  12.3 3.3 %copy-start.3 = (bf16[256,128]{1,0:T(8,128)(2,1)S(1)}, bf16[256,128]{1,0:T(8,128)(2,1)}, u32[]{:S(2)}) copy-start(bf16[256,128]{1,0:T(8,128)(2,1)} %param.5) | copy-start | bytes 196612
  15.7 8.2 %collective-permute-start.3 = (bf16[2,2,256,128]{3,2,1,0:T(8,128)(2,1)S(1)}, bf16[2,2,256,128]{3,2,1,0:T(8,128)(2,1)S(1)}, u32[]{:S(2)}, u32[]{:S(2)}) collective-permute-start(bf16[2,2,256,128]{3,2,1,0:T(8,128)(2,1)S(1)} %get-tuple-element.44), channel_id=1, source_target_pairs={{0,8},{8,0},{16,24},{24,16},{32,40},{40,32},{48,56},{56,48},{64,72... | collective-permute-start | bytes 786440 | tf_op jit(solution)/shard_map/ppermute | solution.py:269
  17.0 6.9 %collective-permute-start.4 = (bf16[2,2,256,128]{3,2,1,0:T(8,128)(2,1)S(1)}, bf16[2,2,256,128]{3,2,1,0:T(8,128)(2,1)S(1)}, u32[]{:S(2)}, u32[]{:S(2)}) collective-permute-start(bf16[2,2,256,128]{3,2,1,0:T(8,128)(2,1)S(1)} %get-tuple-element.43), channel_id=1, source_target_pairs={{0,24},{8,16},{16,8},{24,0},{32,56},{40,48},{48,40},{56,32},{64,88... | collective-permute-start | bytes 786440 | tf_op jit(solution)/shard_map/ppermute | solution.py:270
  18.8 5.0 %collective-permute-start.6 = (bf16[2,256,128]{2,1,0:T(8,128)(2,1)S(1)}, bf16[2,256,128]{2,1,0:T(8,128)(2,1)S(1)}, u32[]{:S(2)}, u32[]{:S(2)}) collective-permute-start(bf16[2,256,128]{2,1,0:T(8,128)(2,1)S(1)} %collective-permute-done.5.refs_5_), channel_id=1, source_target_pairs={{0,32},{8,40},{16,48},{24,56},{32,64},{40,72},{48,80},{56,88},{64,... | collective-permute-start | bytes 393224 | tf_op jit(solution)/shard_map/ppermute | solution.py:271
  24.8 6.1 %collective-permute-start.9 = (bf16[64,1024]{1,0:T(8,128)(2,1)S(1)}, bf16[64,1024]{1,0:T(8,128)(2,1)S(1)}, u32[]{:S(2)}, u32[]{:S(2)}) collective-permute-start(bf16[64,1024]{1,0:T(8,128)(2,1)S(1)} %get-tuple-element.40), channel_id=1, source_target_pairs={{0,6},{1,7},{2,4},{3,5},{4,2},{5,3},{6,0},{7,1},{8,14},{9,15},{10,... | collective-permute-start | bytes 393224 | tf_op jit(solution)/shard_map/ppermute | solution.py:235
  27.7 5.3 %collective-permute-start.8 = (bf16[64,1024]{1,0:T(8,128)(2,1)S(1)}, bf16[64,1024]{1,0:T(8,128)(2,1)S(1)}, u32[]{:S(2)}, u32[]{:S(2)}) collective-permute-start(bf16[64,1024]{1,0:T(8,128)(2,1)S(1)} %get-tuple-element.39), channel_id=1, source_target_pairs={{0,4},{1,5},{2,6},{3,7},{4,0},{5,1},{6,2},{7,3},{8,12},{9,13},{10,... | collective-permute-start | bytes 393224 | tf_op jit(solution)/shard_map/ppermute | solution.py:235
  28.0 5.0 %collective-permute-start.7 = (bf16[64,1024]{1,0:T(8,128)(2,1)S(1)}, bf16[64,1024]{1,0:T(8,128)(2,1)S(1)}, u32[]{:S(2)}, u32[]{:S(2)}) collective-permute-start(bf16[64,1024]{1,0:T(8,128)(2,1)S(1)} %get-tuple-element.38), channel_id=1, source_target_pairs={{0,2},{1,3},{2,0},{3,1},{4,6},{5,7},{6,4},{7,5},{8,10},{9,11},{10,... | collective-permute-start | bytes 393224 | tf_op jit(solution)/shard_map/ppermute | solution.py:235
  33.1 7.9 %collective-permute-start.10 = (bf16[4,32,1024]{2,1,0:T(8,128)(2,1)S(1)}, bf16[4,32,1024]{2,1,0:T(8,128)(2,1)S(1)}, u32[]{:S(2)}, u32[]{:S(2)}) collective-permute-start(bf16[4,32,1024]{2,1,0:T(8,128)(2,1)S(1)} %pad_maximum_fusion.2), channel_id=1, source_target_pairs={{0,1},{1,0},{2,3},{3,2},{4,5},{5,4},{6,7},{7,6},{8,9},{9,8},{10,11... | collective-permute-start | bytes 786440 | tf_op jit(solution)/shard_map/ppermute | solution.py:237

commit v5 on v4

--- a/solution.py
+++ b/solution.py
@@ -255,11 +255,11 @@
     x = place % NX
     send = functools.partial(lax.ppermute, axis_name="ctx")
     own = jnp.stack([keys, values])
-    one = send(own, perm=down)
+    one = jnp.stack([send(keys, perm=down), send(values, perm=down)])
     across = send(own, perm=flip(2))
     two = send(one, perm=down)
     p_one = ((("z", 1),), one)
-    across, mine = lax.optimization_barrier((across, own))
+    one, mine = lax.optimization_barrier((one, own))
     p_own = ((("z", 0),), mine)
     *state, qp, qa = attend_part(doc_lengths, (queries,), [p_own])
     two, state = lax.optimization_barrier((two, state))

time: 42.1 us -> 41.1 us (0.976)
  waiting for transfers between devices: 16.2 us -> 12.7 us
  starting transfers between devices: 18.7 us -> 22.1 us
  local copies, waits for them, and re-layouts: 1.63 us -> 0.67 us
    ppermute x1, starting transfers between devices: 0.08 us -> 2.53 us  [per_device(): one_across = send(across, perm=down)]
    ppermute x1 -> x2, waiting for transfers between devices: 4.42 us -> 2.01 us  [per_device(): one = jnp.stack([send(keys, perm=down), send(values, perm=down)])]
    ppermute x1 -> x2, starting transfers between devices: 2.54 us -> 4.1 us  [per_device(): one = jnp.stack([send(keys, perm=down), send(values, perm=down)])]
    ppermute x1, waiting for transfers between devices: 1.72 us -> 0.25 us  [per_device(): two = send(one, perm=down)]
    unnamed x8, local copies, waits for them, and re-layouts: 1.61 us -> 0.65 us
    ppermute x1, starting transfers between devices: 6.72 us -> 5.99 us  [exchange(): got = lax.ppermute(jnp.stack([h[SHARE:] for h in held]), 'kvh', flip(1))]
    ppermute x1, waiting for transfers between devices: 0.01 us -> 0.43 us  [per_device(): one_across = send(across, perm=down)]
  transfers between devices with their start and end apart: 11 -> 12, of which waited for: 6 -> 8; matrix products, arithmetic and copies ran while one was open for 0% -> 2% of each run, Pallas kernels for 6% -> 6%
where the time goes in v5:
time: 41.1 us; the launch traced here: 41 us
  starting transfers between devices  22.1 us (54%)
  waiting for transfers between devices  12.7 us (31%)
  Pallas kernels  4.17 us (10%)
  other arithmetic  1 us (2%)
  local copies, waits for them, and re-layouts  0.67 us (2%)
    ppermute x1, starting transfers between devices, exchange(): got = lax.ppermute(jnp.stack([h[SHARE:] for h in held]), 'kvh', flip(1))  5.99 us
    ppermute x3, waiting for transfers between devices, exchange(): held[d] = lax.ppermute(pieces[d], 'kvh', flip(2 * d))  4.63 us
    ppermute x1, waiting for transfers between devices, per_device(): two_across = send(one_across, perm=down)  4.21 us
    ppermute x2, starting transfers between devices, per_device(): one = jnp.stack([send(keys, perm=down), send(values, perm=down)])  4.1 us
    ppermute x3, starting transfers between devices, exchange(): held[d] = lax.ppermute(pieces[d], 'kvh', flip(2 * d))  3.5 us
    pallas_call x3, Pallas kernels, attend_part(): pl.pallas_call(functools.partial(attend, kinds, opening, final), out_shap...  3.32 us
    ppermute x1, starting transfers between devices, per_device(): across = send(own, perm=flip(2))  2.83 us
    ppermute x1, starting transfers between devices, per_device(): one_across = send(across, perm=down)  2.53 us
  transfers between devices with their start and end apart: 12, of which 8 were waited for; matrix products, arithmetic and copies ran while one was open for 2% of the time, Pallas kernels for 6%

profile of v5, /device:TPU:1, one launch (start us, length us, event | category | flops | bytes accessed | tf_op | source)
XLA Modules:
  0.0 41.0 jit_solution(15149675203622517451)
XLA Ops:
  0.0 2.5 %collective-permute-start = (bf16[256,128]{1,0:T(8,128)(2,1)}, bf16[256,128]{1,0:T(8,128)(2,1)S(1)}, u32[]{:S(2)}, u32[]{:S(2)}) collective-permute-start(bf16[256,128]{1,0:T(8,128)(2,1)} %param.5), channel_id=1, source_target_pairs={{0,32},{8,40},{16,48},{24,56},{32,64},{40,72},{48,80},{56,88},{64,... | collective-permute-start | bytes 196616 | tf_op jit(solution)/shard_map/ppermute | solution.py:258
  2.5 1.6 %collective-permute-start.1 = (bf16[256,128]{1,0:T(8,128)(2,1)}, bf16[256,128]{1,0:T(8,128)(2,1)S(1)}, u32[]{:S(2)}, u32[]{:S(2)}) collective-permute-start(bf16[256,128]{1,0:T(8,128)(2,1)} %param.6), channel_id=1, source_target_pairs={{0,32},{8,40},{16,48},{24,56},{32,64},{40,72},{48,80},{56,88},{64,... | collective-permute-start | bytes 196616 | tf_op jit(solution)/shard_map/ppermute | solution.py:258
  4.1 0.9 %pad_maximum_fusion.4.refs_2_ = bf16[2,256,128]{2,1,0:T(8,128)(2,1)S(1)} fusion(bf16[1,256,128]{2,1,0:T(8,128)(2,1)} %bitcast.18, bf16[1,256,128]{2,1,0:T(8,128)(2,1)} %bitcast.20), kind=kLoop, calls=%fused_computation.4 | loop fusion | flops 65536 | bytes 262144 | tf_op jit(solution)/shard_map/stack | solution.py:257
  5.0 2.8 %collective-permute-start.5 = (bf16[2,256,128]{2,1,0:T(8,128)(2,1)S(1)}, bf16[2,256,128]{2,1,0:T(8,128)(2,1)S(1)}, u32[]{:S(2)}, u32[]{:S(2)}) collective-permute-start(bf16[2,256,128]{2,1,0:T(8,128)(2,1)S(1)} %pad_maximum_fusion.4.refs_2_), channel_id=1, source_target_pairs={{0,16},{8,24},{16,0},{24,8},{32,48},{40,56},{48,32},{56,40},{64,80... | collective-permute-start | bytes 393224 | tf_op jit(solution)/shard_map/ppermute | solution.py:259
  7.8 0.4 %collective-permute-done = bf16[256,128]{1,0:T(8,128)(2,1)S(1)} collective-permute-done((bf16[256,128]{1,0:T(8,128)(2,1)}, bf16[256,128]{1,0:T(8,128)(2,1)S(1)}, u32[]{:S(2)}, u32[]{:S(2)}) %collective-permute-start) | collective-permute-done | bytes 65568 | tf_op jit(solution)/shard_map/ppermute | solution.py:258
  8.3 1.6 %collective-permute-done.1 = bf16[256,128]{1,0:T(8,128)(2,1)S(1)} collective-permute-done((bf16[256,128]{1,0:T(8,128)(2,1)}, bf16[256,128]{1,0:T(8,128)(2,1)S(1)}, u32[]{:S(2)}, u32[]{:S(2)}) %collective-permute-start.1) | collective-permute-done | bytes 65568 | tf_op jit(solution)/shard_map/ppermute | solution.py:258
  10.0 0.6 %copy-done.1 = s32[16]{0:T(128)S(1)} copy-done((s32[16]{0:T(128)S(1)}, s32[16]{0:T(128)}, u32[]{:S(2)}) %copy-start.1) | copy-done | bytes 88
  10.6 1.5 %attend.3 = (f32[8,256,128]{2,1,0:T(8,128)S(1)}, f32[8,256,128]{2,1,0:T(8,128)S(1)}, f32[8,256,128]{2,1,0:T(8,128)S(1)}, bf16[256,1024]{1,0:T(8,128)(2,1)S(1)}, bf16[256,128]{1,0:T(8,128)(2,1)S(1)}) custom-call(s32[16]{0:T(128)S(1)} %copy-done.1, bf16[256,1024]{1,0:T(8,128)(2,1)S(1)} %copy-done, bf16[2,256,128]{2,1,0:T(8,128)(2,1)S(1)} %pad_maximum_fusion.4.refs_2_), custom_call_target="tpu_custom_call" | custom-call | flops 536870912 | bytes 1048576 | tf_op jit(solution)/shard_map/attend/pallas_call | solution.py:198
  12.2 2.5 %collective-permute-start.6 = (bf16[2,256,128]{2,1,0:T(8,128)(2,1)S(1)}, bf16[2,256,128]{2,1,0:T(8,128)(2,1)S(1)}, u32[]{:S(2)}, u32[]{:S(2)}) collective-permute-start(bf16[2,256,128]{2,1,0:T(8,128)(2,1)S(1)} %collective-permute-done.5.refs_5_), channel_id=1, source_target_pairs={{0,32},{8,40},{16,48},{24,56},{32,64},{40,72},{48,80},{56,88},{64,... | collective-permute-start | bytes 393224 | tf_op jit(solution)/shard_map/ppermute | solution.py:266
  14.7 0.2 collective-permute-done.2.refs_4_
  15.0 1.3 %collective-permute-start.3 = (bf16[2,2,256,128]{3,2,1,0:T(8,128)(2,1)S(1)}, bf16[2,2,256,128]{3,2,1,0:T(8,128)(2,1)S(1)}, u32[]{:S(2)}, u32[]{:S(2)}) collective-permute-start(bf16[2,2,256,128]{3,2,1,0:T(8,128)(2,1)S(1)} %get-tuple-element.44), channel_id=1, source_target_pairs={{0,8},{8,0},{16,24},{24,16},{32,40},{40,32},{48,56},{56,48},{64,72... | collective-permute-start | bytes 786440 | tf_op jit(solution)/shard_map/ppermute | solution.py:269
  16.3 1.8 %collective-permute-start.4 = (bf16[2,2,256,128]{3,2,1,0:T(8,128)(2,1)S(1)}, bf16[2,2,256,128]{3,2,1,0:T(8,128)(2,1)S(1)}, u32[]{:S(2)}, u32[]{:S(2)}) collective-permute-start(bf16[2,2,256,128]{3,2,1,0:T(8,128)(2,1)S(1)} %get-tuple-element.43), channel_id=1, source_target_pairs={{0,24},{8,16},{16,8},{24,0},{32,56},{40,48},{48,40},{56,32},{64,88... | collective-permute-start | bytes 786440 | tf_op jit(solution)/shard_map/ppermute | solution.py:270
  18.2 0.4 %collective-permute-done.6.refs_5_ = bf16[2,256,128]{2,1,0:T(8,128)(2,1)S(1)} collective-permute-done((bf16[2,256,128]{2,1,0:T(8,128)(2,1)S(1)}, bf16[2,256,128]{2,1,0:T(8,128)(2,1)S(1)}, u32[]{:S(2)}, u32[]{:S(2)}) %collective-permute-start.6) | collective-permute-done | bytes 131104 | tf_op jit(solution)/shard_map/ppermute | solution.py:266
  18.6 0.8 %attend.4 = (f32[8,256,128]{2,1,0:T(8,128)S(1)}, f32[8,256,128]{2,1,0:T(8,128)S(1)}, f32[8,256,128]{2,1,0:T(8,128)S(1)}) custom-call(s32[16]{0:T(128)S(1)} %copy-done.1, bf16[256,1024]{1,0:T(8,128)(2,1)S(1)} %get-tuple-element.24.refs_1_, bf16[256,128]{1,0:T(8,128)(2,1)S(1)} %get-tuple-element.25.refs_2_, ...), custom_call_target="tpu_custom_call" | custom-call | flops 1610612736 | bytes 1048576 | tf_op jit(solution)/shard_map/attend/pallas_call | solution.py:198
  19.4 4.2 %collective-permute-done.7.refs_6_ = bf16[2,256,128]{2,1,0:T(8,128)(2,1)S(1)} collective-permute-done((bf16[2,256,128]{2,1,0:T(8,128)(2,1)S(1)}, bf16[2,256,128]{2,1,0:T(8,128)(2,1)S(1)}, u32[]{:S(2)}, u32[]{:S(2)}) %collective-permute-start.7) | collective-permute-done | bytes 131104 | tf_op jit(solution)/shard_map/ppermute | solution.py:271
  23.6 1.0 %attend.5 = (bf16[64,1024]{1,0:T(8,128)(2,1)S(1)}, bf16[64,1024]{1,0:T(8,128)(2,1)S(1)}, bf16[64,1024]{1,0:T(8,128)(2,1)S(1)}, bf16[64,1024]{1,0:T(8,128)(2,1)S(1)}) custom-call(s32[16]{0:T(128)S(1)} %copy-done.1, bf16[256,1024]{1,0:T(8,128)(2,1)S(1)} %get-tuple-element.24.refs_1_, bf16[256,128]{1,0:T(8,128)(2,1)S(1)} %get-tuple-element.25.refs_2_, ...), custom_call_target="tpu_custom_call" | custom-call | flops 2684354560 | bytes 1048576 | tf_op jit(solution)/shard_map/attend/pallas_call | solution.py:198
  24.6 2.8 %collective-permute-start.10 = (bf16[64,1024]{1,0:T(8,128)(2,1)S(1)}, bf16[64,1024]{1,0:T(8,128)(2,1)S(1)}, u32[]{:S(2)}, u32[]{:S(2)}) collective-permute-start(bf16[64,1024]{1,0:T(8,128)(2,1)S(1)} %get-tuple-element.40), channel_id=1, source_target_pairs={{0,6},{1,7},{2,4},{3,5},{4,2},{5,3},{6,0},{7,1},{8,14},{9,15},{10,... | collective-permute-start | bytes 393224 | tf_op jit(solution)/shard_map/ppermute | solution.py:235
  27.4 0.3 collective-permute-start.9
  27.8 0.3 collective-permute-start.8
  28.1 2.6 %collective-permute-done.10.refs_3_ = bf16[64,1024]{1,0:T(8,128)(2,1)S(1)} collective-permute-done((bf16[64,1024]{1,0:T(8,128)(2,1)S(1)}, bf16[64,1024]{1,0:T(8,128)(2,1)S(1)}, u32[]{:S(2)}, u32[]{:S(2)}) %collective-permute-start.10) | collective-permute-done | bytes 131104 | tf_op jit(solution)/shard_map/ppermute | solution.py:235
  30.7 2.0 %collective-permute-done.9.refs_2_ = bf16[64,1024]{1,0:T(8,128)(2,1)S(1)} collective-permute-done((bf16[64,1024]{1,0:T(8,128)(2,1)S(1)}, bf16[64,1024]{1,0:T(8,128)(2,1)S(1)}, u32[]{:S(2)}, u32[]{:S(2)}) %collective-permute-start.9) | collective-permute-done | bytes 131104 | tf_op jit(solution)/shard_map/ppermute | solution.py:235
  32.8 6.0 %collective-permute-start.11 = (bf16[4,32,1024]{2,1,0:T(8,128)(2,1)S(1)}, bf16[4,32,1024]{2,1,0:T(8,128)(2,1)S(1)}, u32[]{:S(2)}, u32[]{:S(2)}) collective-permute-start(bf16[4,32,1024]{2,1,0:T(8,128)(2,1)S(1)} %pad_maximum_fusion.2), channel_id=1, source_target_pairs={{0,1},{1,0},{2,3},{3,2},{4,5},{5,4},{6,7},{7,6},{8,9},{9,8},{10,11... | collective-permute-start | bytes 786440 | tf_op jit(solution)/shard_map/ppermute | solution.py:237
  38.8 1.2 %collective-permute-done.11.refs_4_ = bf16[4,32,1024]{2,1,0:T(8,128)(2,1)S(1)} collective-permute-done((bf16[4,32,1024]{2,1,0:T(8,128)(2,1)S(1)}, bf16[4,32,1024]{2,1,0:T(8,128)(2,1)S(1)}, u32[]{:S(2)}, u32[]{:S(2)}) %collective-permute-start.11) | collective-permute-done | bytes 262176 | tf_op jit(solution)/shard_map/ppermute | solution.py:237
  40.0 0.8 %lay_out.1 = bf16[32,8192]{1,0:T(8,128)(2,1)} custom-call(bf16[64,1024]{1,0:T(8,128)(2,1)S(1)} %get-tuple-element.37.refs_0_, bf16[64,1024]{1,0:T(8,128)(2,1)S(1)} %collective-permute-done.8.refs_1_, bf16[64,1024]{1,0:T(8,128)(2,1)S(1)} %collective-permute-done.9.refs_2_, bf16[64,1024]{1,0:T(8,128)(2,1)S(1)} %collective-permute-done.10.refs_3_, ...), custom_call_target="tpu_custom_call" | custom-call | tf_op jit(solution)/shard_map/lay_out/pallas_call | solution.py:239
  (21 shorter events, 0.3 us)
Async XLA Ops:
  0.0 10.0 %copy-start = (bf16[256,1024]{1,0:T(8,128)(2,1)S(1)}, bf16[256,1024]{1,0:T(8,128)(2,1)}, u32[]{:S(2)}) copy-start(bf16[256,1024]{1,0:T(8,128)(2,1)} %refs_1_.1) | copy-start | bytes 1572868
  0.0 8.3 %collective-permute-start = (bf16[256,128]{1,0:T(8,128)(2,1)}, bf16[256,128]{1,0:T(8,128)(2,1)S(1)}, u32[]{:S(2)}, u32[]{:S(2)}) collective-permute-start(bf16[256,128]{1,0:T(8,128)(2,1)} %param.5), channel_id=1, source_target_pairs={{0,32},{8,40},{16,48},{24,56},{32,64},{40,72},{48,80},{56,88},{64,... | collective-permute-start | bytes 196616 | tf_op jit(solution)/shard_map/ppermute | solution.py:258
  2.5 7.4 %collective-permute-start.1 = (bf16[256,128]{1,0:T(8,128)(2,1)}, bf16[256,128]{1,0:T(8,128)(2,1)S(1)}, u32[]{:S(2)}, u32[]{:S(2)}) collective-permute-start(bf16[256,128]{1,0:T(8,128)(2,1)} %param.6), channel_id=1, source_target_pairs={{0,32},{8,40},{16,48},{24,56},{32,64},{40,72},{48,80},{56,88},{64,... | collective-permute-start | bytes 196616 | tf_op jit(solution)/shard_map/ppermute | solution.py:258
  5.0 7.2 %collective-permute-start.5 = (bf16[2,256,128]{2,1,0:T(8,128)(2,1)S(1)}, bf16[2,256,128]{2,1,0:T(8,128)(2,1)S(1)}, u32[]{:S(2)}, u32[]{:S(2)}) collective-permute-start(bf16[2,256,128]{2,1,0:T(8,128)(2,1)S(1)} %pad_maximum_fusion.4.refs_2_), channel_id=1, source_target_pairs={{0,16},{8,24},{16,0},{24,8},{32,48},{40,56},{48,32},{56,40},{64,80... | collective-permute-start | bytes 393224 | tf_op jit(solution)/shard_map/ppermute | solution.py:259
  9.9 5.1 %collective-permute-start.2 = (bf16[2,256,128]{2,1,0:T(8,128)(2,1)S(1)}, bf16[2,256,128]{2,1,0:T(8,128)(2,1)S(1)}, u32[]{:S(2)}, u32[]{:S(2)}) collective-permute-start(bf16[2,256,128]{2,1,0:T(8,128)(2,1)S(1)} %pad_maximum_fusion.3.refs_3_), channel_id=1, source_target_pairs={{0,32},{8,40},{16,48},{24,56},{32,64},{40,72},{48,80},{56,88},{64,... | collective-permute-start | bytes 393224 | tf_op jit(solution)/shard_map/ppermute | solution.py:260
  10.0 0.7 %copy-start.1 = (s32[16]{0:T(128)S(1)}, s32[16]{0:T(128)}, u32[]{:S(2)}) copy-start(s32[16]{0:T(128)} %refs_0_.5) | copy-start | bytes 196
  10.6 4.3 %copy-start.2 = (bf16[256,128]{1,0:T(8,128)(2,1)S(1)}, bf16[256,128]{1,0:T(8,128)(2,1)}, u32[]{:S(2)}) copy-start(bf16[256,128]{1,0:T(8,128)(2,1)} %param.6) | copy-start | bytes 196612
  10.6 4.3 %copy-start.3 = (bf16[256,128]{1,0:T(8,128)(2,1)S(1)}, bf16[256,128]{1,0:T(8,128)(2,1)}, u32[]{:S(2)}) copy-start(bf16[256,128]{1,0:T(8,128)(2,1)} %param.5) | copy-start | bytes 196612
  12.2 6.4 %collective-permute-start.6 = (bf16[2,256,128]{2,1,0:T(8,128)(2,1)S(1)}, bf16[2,256,128]{2,1,0:T(8,128)(2,1)S(1)}, u32[]{:S(2)}, u32[]{:S(2)}) collective-permute-start(bf16[2,256,128]{2,1,0:T(8,128)(2,1)S(1)} %collective-permute-done.5.refs_5_), channel_id=1, source_target_pairs={{0,32},{8,40},{16,48},{24,56},{32,64},{40,72},{48,80},{56,88},{64,... | collective-permute-start | bytes 393224 | tf_op jit(solution)/shard_map/ppermute | solution.py:266
  15.0 8.6 %collective-permute-start.3 = (bf16[2,2,256,128]{3,2,1,0:T(8,128)(2,1)S(1)}, bf16[2,2,256,128]{3,2,1,0:T(8,128)(2,1)S(1)}, u32[]{:S(2)}, u32[]{:S(2)}) collective-permute-start(bf16[2,2,256,128]{3,2,1,0:T(8,128)(2,1)S(1)} %get-tuple-element.44), channel_id=1, source_target_pairs={{0,8},{8,0},{16,24},{24,16},{32,40},{40,32},{48,56},{56,48},{64,72... | collective-permute-start | bytes 786440 | tf_op jit(solution)/shard_map/ppermute | solution.py:269
  16.3 7.3 %collective-permute-start.4 = (bf16[2,2,256,128]{3,2,1,0:T(8,128)(2,1)S(1)}, bf16[2,2,256,128]{3,2,1,0:T(8,128)(2,1)S(1)}, u32[]{:S(2)}, u32[]{:S(2)}) collective-permute-start(bf16[2,2,256,128]{3,2,1,0:T(8,128)(2,1)S(1)} %get-tuple-element.43), channel_id=1, source_target_pairs={{0,24},{8,16},{16,8},{24,0},{32,56},{40,48},{48,40},{56,32},{64,88... | collective-permute-start | bytes 786440 | tf_op jit(solution)/shard_map/ppermute | solution.py:270
  18.6 5.0 %collective-permute-start.7 = (bf16[2,256,128]{2,1,0:T(8,128)(2,1)S(1)}, bf16[2,256,128]{2,1,0:T(8,128)(2,1)S(1)}, u32[]{:S(2)}, u32[]{:S(2)}) collective-permute-start(bf16[2,256,128]{2,1,0:T(8,128)(2,1)S(1)} %collective-permute-done.6.refs_5_), channel_id=1, source_target_pairs={{0,32},{8,40},{16,48},{24,56},{32,64},{40,72},{48,80},{56,88},{64,... | collective-permute-start | bytes 393224 | tf_op jit(solution)/shard_map/ppermute | solution.py:271
  24.6 6.1 %collective-permute-start.10 = (bf16[64,1024]{1,0:T(8,128)(2,1)S(1)}, bf16[64,1024]{1,0:T(8,128)(2,1)S(1)}, u32[]{:S(2)}, u32[]{:S(2)}) collective-permute-start(bf16[64,1024]{1,0:T(8,128)(2,1)S(1)} %get-tuple-element.40), channel_id=1, source_target_pairs={{0,6},{1,7},{2,4},{3,5},{4,2},{5,3},{6,0},{7,1},{8,14},{9,15},{10,... | collective-permute-start | bytes 393224 | tf_op jit(solution)/shard_map/ppermute | solution.py:235
  27.4 5.3 %collective-permute-start.9 = (bf16[64,1024]{1,0:T(8,128)(2,1)S(1)}, bf16[64,1024]{1,0:T(8,128)(2,1)S(1)}, u32[]{:S(2)}, u32[]{:S(2)}) collective-permute-start(bf16[64,1024]{1,0:T(8,128)(2,1)S(1)} %get-tuple-element.39), channel_id=1, source_target_pairs={{0,4},{1,5},{2,6},{3,7},{4,0},{5,1},{6,2},{7,3},{8,12},{9,13},{10,... | collective-permute-start | bytes 393224 | tf_op jit(solution)/shard_map/ppermute | solution.py:235
  27.8 5.0 %collective-permute-start.8 = (bf16[64,1024]{1,0:T(8,128)(2,1)S(1)}, bf16[64,1024]{1,0:T(8,128)(2,1)S(1)}, u32[]{:S(2)}, u32[]{:S(2)}) collective-permute-start(bf16[64,1024]{1,0:T(8,128)(2,1)S(1)} %get-tuple-element.38), channel_id=1, source_target_pairs={{0,2},{1,3},{2,0},{3,1},{4,6},{5,7},{6,4},{7,5},{8,10},{9,11},{10,... | collective-permute-start | bytes 393224 | tf_op jit(solution)/shard_map/ppermute | solution.py:235
  32.8 7.2 %collective-permute-start.11 = (bf16[4,32,1024]{2,1,0:T(8,128)(2,1)S(1)}, bf16[4,32,1024]{2,1,0:T(8,128)(2,1)S(1)}, u32[]{:S(2)}, u32[]{:S(2)}) collective-permute-start(bf16[4,32,1024]{2,1,0:T(8,128)(2,1)S(1)} %pad_maximum_fusion.2), channel_id=1, source_target_pairs={{0,1},{1,0},{2,3},{3,2},{4,5},{5,4},{6,7},{7,6},{8,9},{9,8},{10,11... | collective-permute-start | bytes 786440 | tf_op jit(solution)/shard_map/ppermute | solution.py:237

commit v6 on v5

--- a/solution.py
+++ b/solution.py
@@ -259,11 +259,11 @@
     across = send(own, perm=flip(2))
     two = send(one, perm=down)
     p_one = ((("z", 1),), one)
-    one, mine = lax.optimization_barrier((one, own))
+    one_across = send(one, perm=flip(2))
+    one, mine, across = lax.optimization_barrier((one, own, across))
     p_own = ((("z", 0),), mine)
     *state, qp, qa = attend_part(doc_lengths, (queries,), [p_own])
     two, state = lax.optimization_barrier((two, state))
-    one_across = send(across, perm=down)
     low = jnp.stack([one, jnp.where(x & 1 == 0, own, two)])
     high = jnp.stack([one, jnp.where(x & 2 == 0, own, two)])
     near = send(low, perm=flip(1))

time: 41.1 us -> 40.3 us (0.981)
  local copies, waits for them, and re-layouts: 0.67 us -> 0.04 us
    ppermute x1, starting transfers between devices: 5.99 us -> 5.29 us  [exchange(): got = lax.ppermute(jnp.stack([h[SHARE:] for h in held]), 'kvh', flip(1))]
    unnamed x8, local copies, waits for them, and re-layouts: 0.65 us -> 0.02 us
    ppermute x1, waiting for transfers between devices: 0.43 us -> 0.01 us  [per_device(): one_across = send(one, perm=flip(2))]
  transfers between devices with their start and end apart: 12 -> 12, of which waited for: 8 -> 7; matrix products, arithmetic and copies ran while one was open for 2% -> 2% of each run, Pallas kernels for 6% -> 6%
where the time goes in v6:
time: 40.3 us; the launch traced here: 40.2 us
  starting transfers between devices  21.8 us (54%)
  waiting for transfers between devices  12.9 us (32%)
  Pallas kernels  4.17 us (10%)
  other arithmetic  1 us (2%)
    ppermute x1, starting transfers between devices, exchange(): got = lax.ppermute(jnp.stack([h[SHARE:] for h in held]), 'kvh', flip(1))  5.29 us
    ppermute x3, waiting for transfers between devices, exchange(): held[d] = lax.ppermute(pieces[d], 'kvh', flip(2 * d))  4.65 us
    ppermute x1, waiting for transfers between devices, per_device(): two_across = send(one_across, perm=down)  4.51 us
    ppermute x2, starting transfers between devices, per_device(): one = jnp.stack([send(keys, perm=down), send(values, perm=down)])  4.1 us
    ppermute x3, starting transfers between devices, exchange(): held[d] = lax.ppermute(pieces[d], 'kvh', flip(2 * d))  3.5 us
    pallas_call x3, Pallas kernels, attend_part(): pl.pallas_call(functools.partial(attend, kinds, opening, final), out_shap...  3.32 us
    ppermute x1, starting transfers between devices, per_device(): across = send(own, perm=flip(2))  2.83 us
    ppermute x1, starting transfers between devices, per_device(): one_across = send(one, perm=flip(2))  2.83 us
  transfers between devices with their start and end apart: 12, of which 7 were waited for; matrix products, arithmetic and copies ran while one was open for 2% of the time, Pallas kernels for 6%

profile of v6, /device:TPU:1, one launch (start us, length us, event | category | flops | bytes accessed | tf_op | source)
XLA Modules:
  0.0 40.2 jit_solution(2126828399080952007)
XLA Ops:
  0.0 2.5 %collective-permute-start = (bf16[256,128]{1,0:T(8,128)(2,1)}, bf16[256,128]{1,0:T(8,128)(2,1)S(1)}, u32[]{:S(2)}, u32[]{:S(2)}) collective-permute-start(bf16[256,128]{1,0:T(8,128)(2,1)} %param.5), channel_id=1, source_target_pairs={{0,32},{8,40},{16,48},{24,56},{32,64},{40,72},{48,80},{56,88},{64,... | collective-permute-start | bytes 196616 | tf_op jit(solution)/shard_map/ppermute | solution.py:258
  2.5 1.6 %collective-permute-start.1 = (bf16[256,128]{1,0:T(8,128)(2,1)}, bf16[256,128]{1,0:T(8,128)(2,1)S(1)}, u32[]{:S(2)}, u32[]{:S(2)}) collective-permute-start(bf16[256,128]{1,0:T(8,128)(2,1)} %param.6), channel_id=1, source_target_pairs={{0,32},{8,40},{16,48},{24,56},{32,64},{40,72},{48,80},{56,88},{64,... | collective-permute-start | bytes 196616 | tf_op jit(solution)/shard_map/ppermute | solution.py:258
  4.1 0.9 %pad_maximum_fusion.4.refs_2_ = bf16[2,256,128]{2,1,0:T(8,128)(2,1)S(1)} fusion(bf16[1,256,128]{2,1,0:T(8,128)(2,1)} %bitcast.18, bf16[1,256,128]{2,1,0:T(8,128)(2,1)} %bitcast.20), kind=kLoop, calls=%fused_computation.4 | loop fusion | flops 65536 | bytes 262144 | tf_op jit(solution)/shard_map/stack | solution.py:257
  5.0 2.8 %collective-permute-start.2 = (bf16[2,256,128]{2,1,0:T(8,128)(2,1)S(1)}, bf16[2,256,128]{2,1,0:T(8,128)(2,1)S(1)}, u32[]{:S(2)}, u32[]{:S(2)}) collective-permute-start(bf16[2,256,128]{2,1,0:T(8,128)(2,1)S(1)} %pad_maximum_fusion.4.refs_2_), channel_id=1, source_target_pairs={{0,16},{8,24},{16,0},{24,8},{32,48},{40,56},{48,32},{56,40},{64,80... | collective-permute-start | bytes 393224 | tf_op jit(solution)/shard_map/ppermute | solution.py:259
  7.8 0.4 %collective-permute-done = bf16[256,128]{1,0:T(8,128)(2,1)S(1)} collective-permute-done((bf16[256,128]{1,0:T(8,128)(2,1)}, bf16[256,128]{1,0:T(8,128)(2,1)S(1)}, u32[]{:S(2)}, u32[]{:S(2)}) %collective-permute-start) | collective-permute-done | bytes 65568 | tf_op jit(solution)/shard_map/ppermute | solution.py:258
  8.3 1.6 %collective-permute-done.1 = bf16[256,128]{1,0:T(8,128)(2,1)S(1)} collective-permute-done((bf16[256,128]{1,0:T(8,128)(2,1)}, bf16[256,128]{1,0:T(8,128)(2,1)S(1)}, u32[]{:S(2)}, u32[]{:S(2)}) %collective-permute-start.1) | collective-permute-done | bytes 65568 | tf_op jit(solution)/shard_map/ppermute | solution.py:258
  9.9 0.1 collective-permute-start.3
  10.0 0.0 copy-start.2
  10.0 2.8 %collective-permute-start.6 = (bf16[2,256,128]{2,1,0:T(8,128)(2,1)S(1)}, bf16[2,256,128]{2,1,0:T(8,128)(2,1)S(1)}, u32[]{:S(2)}, u32[]{:S(2)}) collective-permute-start(bf16[2,256,128]{2,1,0:T(8,128)(2,1)S(1)} %pad_maximum_fusion.3.refs_3_), channel_id=1, source_target_pairs={{0,16},{8,24},{16,0},{24,8},{32,48},{40,56},{48,32},{56,40},{64,80... | collective-permute-start | bytes 393224 | tf_op jit(solution)/shard_map/ppermute | solution.py:262
  12.8 1.5 %attend.3 = (f32[8,256,128]{2,1,0:T(8,128)S(1)}, f32[8,256,128]{2,1,0:T(8,128)S(1)}, f32[8,256,128]{2,1,0:T(8,128)S(1)}, bf16[256,1024]{1,0:T(8,128)(2,1)S(1)}, bf16[256,128]{1,0:T(8,128)(2,1)S(1)}) custom-call(s32[16]{0:T(128)S(1)} %copy-done.1, bf16[256,1024]{1,0:T(8,128)(2,1)S(1)} %copy-done, bf16[2,256,128]{2,1,0:T(8,128)(2,1)S(1)} %pad_maximum_fusion.4.refs_2_), custom_call_target="tpu_custom_call" | custom-call | flops 536870912 | bytes 1048576 | tf_op jit(solution)/shard_map/attend/pallas_call | solution.py:198
  14.4 0.6 %collective-permute-done.3.refs_4_ = bf16[2,256,128]{2,1,0:T(8,128)(2,1)S(1)} collective-permute-done((bf16[2,256,128]{2,1,0:T(8,128)(2,1)S(1)}, bf16[2,256,128]{2,1,0:T(8,128)(2,1)S(1)}, u32[]{:S(2)}, u32[]{:S(2)}) %collective-permute-start.3) | collective-permute-done | bytes 131104 | tf_op jit(solution)/shard_map/ppermute | solution.py:260
  15.0 1.3 %collective-permute-start.4 = (bf16[2,2,256,128]{3,2,1,0:T(8,128)(2,1)S(1)}, bf16[2,2,256,128]{3,2,1,0:T(8,128)(2,1)S(1)}, u32[]{:S(2)}, u32[]{:S(2)}) collective-permute-start(bf16[2,2,256,128]{3,2,1,0:T(8,128)(2,1)S(1)} %get-tuple-element.46), channel_id=1, source_target_pairs={{0,8},{8,0},{16,24},{24,16},{32,40},{40,32},{48,56},{56,48},{64,72... | collective-permute-start | bytes 786440 | tf_op jit(solution)/shard_map/ppermute | solution.py:269
  16.3 1.8 %collective-permute-start.5 = (bf16[2,2,256,128]{3,2,1,0:T(8,128)(2,1)S(1)}, bf16[2,2,256,128]{3,2,1,0:T(8,128)(2,1)S(1)}, u32[]{:S(2)}, u32[]{:S(2)}) collective-permute-start(bf16[2,2,256,128]{3,2,1,0:T(8,128)(2,1)S(1)} %get-tuple-element.45), channel_id=1, source_target_pairs={{0,24},{8,16},{16,8},{24,0},{32,56},{40,48},{48,40},{56,32},{64,88... | collective-permute-start | bytes 786440 | tf_op jit(solution)/shard_map/ppermute | solution.py:270
  18.2 0.8 %attend.4 = (f32[8,256,128]{2,1,0:T(8,128)S(1)}, f32[8,256,128]{2,1,0:T(8,128)S(1)}, f32[8,256,128]{2,1,0:T(8,128)S(1)}) custom-call(s32[16]{0:T(128)S(1)} %copy-done.1, bf16[256,1024]{1,0:T(8,128)(2,1)S(1)} %get-tuple-element.25.refs_1_, bf16[256,128]{1,0:T(8,128)(2,1)S(1)} %get-tuple-element.26.refs_2_, ...), custom_call_target="tpu_custom_call" | custom-call | flops 1610612736 | bytes 1048576 | tf_op jit(solution)/shard_map/attend/pallas_call | solution.py:198
  19.0 4.5 %collective-permute-done.7.refs_6_ = bf16[2,256,128]{2,1,0:T(8,128)(2,1)S(1)} collective-permute-done((bf16[2,256,128]{2,1,0:T(8,128)(2,1)S(1)}, bf16[2,256,128]{2,1,0:T(8,128)(2,1)S(1)}, u32[]{:S(2)}, u32[]{:S(2)}) %collective-permute-start.7) | collective-permute-done | bytes 131104 | tf_op jit(solution)/shard_map/ppermute | solution.py:271
  23.5 1.0 %attend.5 = (bf16[64,1024]{1,0:T(8,128)(2,1)S(1)}, bf16[64,1024]{1,0:T(8,128)(2,1)S(1)}, bf16[64,1024]{1,0:T(8,128)(2,1)S(1)}, bf16[64,1024]{1,0:T(8,128)(2,1)S(1)}) custom-call(s32[16]{0:T(128)S(1)} %copy-done.1, bf16[256,1024]{1,0:T(8,128)(2,1)S(1)} %get-tuple-element.25.refs_1_, bf16[256,128]{1,0:T(8,128)(2,1)S(1)} %get-tuple-element.26.refs_2_, ...), custom_call_target="tpu_custom_call" | custom-call | flops 2684354560 | bytes 1048576 | tf_op jit(solution)/shard_map/attend/pallas_call | solution.py:198
  24.5 2.8 %collective-permute-start.10 = (bf16[64,1024]{1,0:T(8,128)(2,1)S(1)}, bf16[64,1024]{1,0:T(8,128)(2,1)S(1)}, u32[]{:S(2)}, u32[]{:S(2)}) collective-permute-start(bf16[64,1024]{1,0:T(8,128)(2,1)S(1)} %get-tuple-element.42), channel_id=1, source_target_pairs={{0,6},{1,7},{2,4},{3,5},{4,2},{5,3},{6,0},{7,1},{8,14},{9,15},{10,... | collective-permute-start | bytes 393224 | tf_op jit(solution)/shard_map/ppermute | solution.py:235
  27.3 0.3 collective-permute-start.9
  27.6 0.3 collective-permute-start.8
  28.0 2.6 %collective-permute-done.10.refs_3_ = bf16[64,1024]{1,0:T(8,128)(2,1)S(1)} collective-permute-done((bf16[64,1024]{1,0:T(8,128)(2,1)S(1)}, bf16[64,1024]{1,0:T(8,128)(2,1)S(1)}, u32[]{:S(2)}, u32[]{:S(2)}) %collective-permute-start.10) | collective-permute-done | bytes 131104 | tf_op jit(solution)/shard_map/ppermute | solution.py:235
  30.6 2.0 %collective-permute-done.9.refs_2_ = bf16[64,1024]{1,0:T(8,128)(2,1)S(1)} collective-permute-done((bf16[64,1024]{1,0:T(8,128)(2,1)S(1)}, bf16[64,1024]{1,0:T(8,128)(2,1)S(1)}, u32[]{:S(2)}, u32[]{:S(2)}) %collective-permute-start.9) | collective-permute-done | bytes 131104 | tf_op jit(solution)/shard_map/ppermute | solution.py:235
  32.7 5.3 %collective-permute-start.11 = (bf16[4,32,1024]{2,1,0:T(8,128)(2,1)S(1)}, bf16[4,32,1024]{2,1,0:T(8,128)(2,1)S(1)}, u32[]{:S(2)}, u32[]{:S(2)}) collective-permute-start(bf16[4,32,1024]{2,1,0:T(8,128)(2,1)S(1)} %pad_maximum_fusion.2), channel_id=1, source_target_pairs={{0,1},{1,0},{2,3},{3,2},{4,5},{5,4},{6,7},{7,6},{8,9},{9,8},{10,11... | collective-permute-start | bytes 786440 | tf_op jit(solution)/shard_map/ppermute | solution.py:237
  38.0 1.2 %collective-permute-done.11.refs_4_ = bf16[4,32,1024]{2,1,0:T(8,128)(2,1)S(1)} collective-permute-done((bf16[4,32,1024]{2,1,0:T(8,128)(2,1)S(1)}, bf16[4,32,1024]{2,1,0:T(8,128)(2,1)S(1)}, u32[]{:S(2)}, u32[]{:S(2)}) %collective-permute-start.11) | collective-permute-done | bytes 262176 | tf_op jit(solution)/shard_map/ppermute | solution.py:237
  39.2 0.8 %lay_out.1 = bf16[32,8192]{1,0:T(8,128)(2,1)} custom-call(bf16[64,1024]{1,0:T(8,128)(2,1)S(1)} %get-tuple-element.39.refs_0_, bf16[64,1024]{1,0:T(8,128)(2,1)S(1)} %collective-permute-done.8.refs_1_, bf16[64,1024]{1,0:T(8,128)(2,1)S(1)} %collective-permute-done.9.refs_2_, bf16[64,1024]{1,0:T(8,128)(2,1)S(1)} %collective-permute-done.10.refs_3_, ...), custom_call_target="tpu_custom_call" | custom-call | tf_op jit(solution)/shard_map/lay_out/pallas_call | solution.py:239
  (21 shorter events, 0.2 us)
Async XLA Ops:
  0.0 12.8 %copy-start = (bf16[256,1024]{1,0:T(8,128)(2,1)S(1)}, bf16[256,1024]{1,0:T(8,128)(2,1)}, u32[]{:S(2)}) copy-start(bf16[256,1024]{1,0:T(8,128)(2,1)} %refs_1_.1) | copy-start | bytes 1572868
  0.0 8.3 %collective-permute-start = (bf16[256,128]{1,0:T(8,128)(2,1)}, bf16[256,128]{1,0:T(8,128)(2,1)S(1)}, u32[]{:S(2)}, u32[]{:S(2)}) collective-permute-start(bf16[256,128]{1,0:T(8,128)(2,1)} %param.5), channel_id=1, source_target_pairs={{0,32},{8,40},{16,48},{24,56},{32,64},{40,72},{48,80},{56,88},{64,... | collective-permute-start | bytes 196616 | tf_op jit(solution)/shard_map/ppermute | solution.py:258
  2.5 7.4 %collective-permute-start.1 = (bf16[256,128]{1,0:T(8,128)(2,1)}, bf16[256,128]{1,0:T(8,128)(2,1)S(1)}, u32[]{:S(2)}, u32[]{:S(2)}) collective-permute-start(bf16[256,128]{1,0:T(8,128)(2,1)} %param.6), channel_id=1, source_target_pairs={{0,32},{8,40},{16,48},{24,56},{32,64},{40,72},{48,80},{56,88},{64,... | collective-permute-start | bytes 196616 | tf_op jit(solution)/shard_map/ppermute | solution.py:258
  5.0 7.8 %collective-permute-start.2 = (bf16[2,256,128]{2,1,0:T(8,128)(2,1)S(1)}, bf16[2,256,128]{2,1,0:T(8,128)(2,1)S(1)}, u32[]{:S(2)}, u32[]{:S(2)}) collective-permute-start(bf16[2,256,128]{2,1,0:T(8,128)(2,1)S(1)} %pad_maximum_fusion.4.refs_2_), channel_id=1, source_target_pairs={{0,16},{8,24},{16,0},{24,8},{32,48},{40,56},{48,32},{56,40},{64,80... | collective-permute-start | bytes 393224 | tf_op jit(solution)/shard_map/ppermute | solution.py:259
  9.9 5.1 %collective-permute-start.3 = (bf16[2,256,128]{2,1,0:T(8,128)(2,1)S(1)}, bf16[2,256,128]{2,1,0:T(8,128)(2,1)S(1)}, u32[]{:S(2)}, u32[]{:S(2)}) collective-permute-start(bf16[2,256,128]{2,1,0:T(8,128)(2,1)S(1)} %pad_maximum_fusion.3.refs_3_), channel_id=1, source_target_pairs={{0,32},{8,40},{16,48},{24,56},{32,64},{40,72},{48,80},{56,88},{64,... | collective-permute-start | bytes 393224 | tf_op jit(solution)/shard_map/ppermute | solution.py:260
  10.0 2.9 %copy-start.1 = (s32[16]{0:T(128)S(1)}, s32[16]{0:T(128)}, u32[]{:S(2)}) copy-start(s32[16]{0:T(128)} %refs_0_.5) | copy-start | bytes 196
  10.0 5.0 %copy-start.2 = (bf16[256,128]{1,0:T(8,128)(2,1)S(1)}, bf16[256,128]{1,0:T(8,128)(2,1)}, u32[]{:S(2)}) copy-start(bf16[256,128]{1,0:T(8,128)(2,1)} %param.6) | copy-start | bytes 196612
  10.0 5.0 %copy-start.3 = (bf16[256,128]{1,0:T(8,128)(2,1)S(1)}, bf16[256,128]{1,0:T(8,128)(2,1)}, u32[]{:S(2)}) copy-start(bf16[256,128]{1,0:T(8,128)(2,1)} %param.5) | copy-start | bytes 196612
  10.0 8.2 %collective-permute-start.6 = (bf16[2,256,128]{2,1,0:T(8,128)(2,1)S(1)}, bf16[2,256,128]{2,1,0:T(8,128)(2,1)S(1)}, u32[]{:S(2)}, u32[]{:S(2)}) collective-permute-start(bf16[2,256,128]{2,1,0:T(8,128)(2,1)S(1)} %pad_maximum_fusion.3.refs_3_), channel_id=1, source_target_pairs={{0,16},{8,24},{16,0},{24,8},{32,48},{40,56},{48,32},{56,40},{64,80... | collective-permute-start | bytes 393224 | tf_op jit(solution)/shard_map/ppermute | solution.py:262
  15.0 8.4 %collective-permute-start.4 = (bf16[2,2,256,128]{3,2,1,0:T(8,128)(2,1)S(1)}, bf16[2,2,256,128]{3,2,1,0:T(8,128)(2,1)S(1)}, u32[]{:S(2)}, u32[]{:S(2)}) collective-permute-start(bf16[2,2,256,128]{3,2,1,0:T(8,128)(2,1)S(1)} %get-tuple-element.46), channel_id=1, source_target_pairs={{0,8},{8,0},{16,24},{24,16},{32,40},{40,32},{48,56},{56,48},{64,72... | collective-permute-start | bytes 786440 | tf_op jit(solution)/shard_map/ppermute | solution.py:269
  16.3 7.2 %collective-permute-start.5 = (bf16[2,2,256,128]{3,2,1,0:T(8,128)(2,1)S(1)}, bf16[2,2,256,128]{3,2,1,0:T(8,128)(2,1)S(1)}, u32[]{:S(2)}, u32[]{:S(2)}) collective-permute-start(bf16[2,2,256,128]{3,2,1,0:T(8,128)(2,1)S(1)} %get-tuple-element.45), channel_id=1, source_target_pairs={{0,24},{8,16},{16,8},{24,0},{32,56},{40,48},{48,40},{56,32},{64,88... | collective-permute-start | bytes 786440 | tf_op jit(solution)/shard_map/ppermute | solution.py:270
  18.2 5.3 %collective-permute-start.7 = (bf16[2,256,128]{2,1,0:T(8,128)(2,1)S(1)}, bf16[2,256,128]{2,1,0:T(8,128)(2,1)S(1)}, u32[]{:S(2)}, u32[]{:S(2)}) collective-permute-start(bf16[2,256,128]{2,1,0:T(8,128)(2,1)S(1)} %collective-permute-done.6.refs_5_), channel_id=1, source_target_pairs={{0,32},{8,40},{16,48},{24,56},{32,64},{40,72},{48,80},{56,88},{64,... | collective-permute-start | bytes 393224 | tf_op jit(solution)/shard_map/ppermute | solution.py:271
  24.5 6.1 %collective-permute-start.10 = (bf16[64,1024]{1,0:T(8,128)(2,1)S(1)}, bf16[64,1024]{1,0:T(8,128)(2,1)S(1)}, u32[]{:S(2)}, u32[]{:S(2)}) collective-permute-start(bf16[64,1024]{1,0:T(8,128)(2,1)S(1)} %get-tuple-element.42), channel_id=1, source_target_pairs={{0,6},{1,7},{2,4},{3,5},{4,2},{5,3},{6,0},{7,1},{8,14},{9,15},{10,... | collective-permute-start | bytes 393224 | tf_op jit(solution)/shard_map/ppermute | solution.py:235
  27.3 5.3 %collective-permute-start.9 = (bf16[64,1024]{1,0:T(8,128)(2,1)S(1)}, bf16[64,1024]{1,0:T(8,128)(2,1)S(1)}, u32[]{:S(2)}, u32[]{:S(2)}) collective-permute-start(bf16[64,1024]{1,0:T(8,128)(2,1)S(1)} %get-tuple-element.41), channel_id=1, source_target_pairs={{0,4},{1,5},{2,6},{3,7},{4,0},{5,1},{6,2},{7,3},{8,12},{9,13},{10,... | collective-permute-start | bytes 393224 | tf_op jit(solution)/shard_map/ppermute | solution.py:235
  27.6 5.0 %collective-permute-start.8 = (bf16[64,1024]{1,0:T(8,128)(2,1)S(1)}, bf16[64,1024]{1,0:T(8,128)(2,1)S(1)}, u32[]{:S(2)}, u32[]{:S(2)}) collective-permute-start(bf16[64,1024]{1,0:T(8,128)(2,1)S(1)} %get-tuple-element.40), channel_id=1, source_target_pairs={{0,2},{1,3},{2,0},{3,1},{4,6},{5,7},{6,4},{7,5},{8,10},{9,11},{10,... | collective-permute-start | bytes 393224 | tf_op jit(solution)/shard_map/ppermute | solution.py:235
  32.7 6.5 %collective-permute-start.11 = (bf16[4,32,1024]{2,1,0:T(8,128)(2,1)S(1)}, bf16[4,32,1024]{2,1,0:T(8,128)(2,1)S(1)}, u32[]{:S(2)}, u32[]{:S(2)}) collective-permute-start(bf16[4,32,1024]{2,1,0:T(8,128)(2,1)S(1)} %pad_maximum_fusion.2), channel_id=1, source_target_pairs={{0,1},{1,0},{2,3},{3,2},{4,5},{5,4},{6,7},{7,6},{8,9},{9,8},{10,11... | collective-permute-start | bytes 786440 | tf_op jit(solution)/shard_map/ppermute | solution.py:237
